TPU v7x, 32 devices: a whole 2x2x4 slice. The times are simulated.
32 devices in a mesh: dp: 4 (over x, core), seq: 2 (over y), mp: 4 (over z).
Axes of the slice: x: 2, y: 2, z: 4, core: 2. Of those that a mesh axis runs over, the one named last changes fastest.
Arguments:
- tokens: bfloat16 [4096, 2304], P(('dp', 'seq')), may hold values from -6 to 6
- gain_attn: bfloat16 [2304], P(('dp', 'seq')), may hold values from 0.5 to 1.5
- w_query: bfloat16 [2304, 2048], P(('dp', 'seq'), 'mp'), may hold values from -0.125 to 0.125
- w_key: bfloat16 [2304, 1024], P(('dp', 'seq'), 'mp'), may hold values from -0.125 to 0.125
- w_value: bfloat16 [2304, 1024], P(('dp', 'seq'), 'mp'), may hold values from -0.125 to 0.125
- w_out: bfloat16 [2048, 2304], P('mp', ('dp', 'seq')), may hold values from -1 to 1
- gain_ffn: bfloat16 [2304], P(('dp', 'seq')), may hold values from 0.5 to 1.5
- w_gate: bfloat16 [2304, 9216], P(('dp', 'seq'), 'mp'), may hold values from -0.125 to 0.125
- w_up: bfloat16 [2304, 9216], P(('dp', 'seq'), 'mp'), may hold values from -0.125 to 0.125
- w_down: bfloat16 [9216, 2304], P('mp', ('dp', 'seq')), may hold values from -0.125 to 0.125
- width_pick: int32 [7], replicated, may hold values from 0 to 2
- segments: int32 [4, 1024], P('dp'), may hold values from 0 to 65, as said below
- cotangent: bfloat16 [4096, 2304], P(('dp', 'seq')), may hold values from -6 to 6
Outputs:
- mixed: float32 [4096, 2304], P(('dp', 'seq'))
- grad_tokens: float32 [4096, 2304], P(('dp', 'seq'))
- grad_query: float32 [2304, 2048], P(('dp', 'seq'), 'mp')
- grad_key: float32 [2304, 1024], P(('dp', 'seq'), 'mp')
- grad_value: float32 [2304, 1024], P(('dp', 'seq'), 'mp')
- grad_out: float32 [2048, 2304], P('mp', ('dp', 'seq'))
- grad_gate: float32 [2304, 9216], P(('dp', 'seq'), 'mp')
- grad_up: float32 [2304, 9216], P(('dp', 'seq'), 'mp')
- grad_down: float32 [9216, 2304], P('mp', ('dp', 'seq'))
- grad_gain_attn: float32 [2304], P(('dp', 'seq'))
- grad_gain_ffn: float32 [2304], P(('dp', 'seq'))
- attn_scales: float32 [2, 2048], P(None, 'mp')
- kv_scales: float32 [2, 1024], P(None, 'mp')
- ffn_scales: float32 [3, 9216], P(None, 'mp')
Inputs may be any that keep to these rules, and one draw needn't show every extreme that they name: `segments`: in each row the numbers start at 0 and rise by one at each new document; one document of each row covers exactly 513 consecutive slots, at the start or at the end of the row, and the other 511 slots hold exactly 65 short documents. `width_pick`: entry i picks the level of the i-th weight in the order query, key, value, out, gate, up, down.
All inputs are finite; a program needn't handle non-finite values.
Results may differ from a plain program's by a relative error of at most 0.013.
Values may be sent and summed in bfloat16 or wider, within the bound.
A program may use at most 256 MiB of HBM per device.

v0:
```python
import jax
import jax.numpy as jnp
from jax import lax
from jax.sharding import PartitionSpec as P

HQ = 8
HK = 4
HD = 256


EPSILON = 1e-06
SOFTCAP = 50.0


def width_levels(width_pick):
    return jnp.where(width_pick == 0, 1.0, jnp.where(width_pick == 1, 0.5, 0.25)).astype(
        jnp.float32
    )


def bounded(weight, bound):
    return (bound * jnp.tanh(weight.astype(jnp.float32) / bound)).astype(jnp.bfloat16)


def bound_slope(weight, bound):
    tangent = jnp.tanh(weight.astype(jnp.float32) / bound)
    return 1.0 - tangent * tangent


def channel_peak(weight, along):
    return jnp.max(jnp.abs(weight.astype(jnp.float32)), axis=along)


def inner_rows(left, right):
    return lax.dot_general(
        left, right, (((0,), (0,)), ((), ())), preferred_element_type=jnp.float32
    )


def against(left, weight):
    return lax.dot_general(
        left, weight, (((1,), (1,)), ((), ())), preferred_element_type=jnp.float32
    )


def forward_norm(values):
    inverse = lax.rsqrt(jnp.mean(values * values, axis=-1, keepdims=True) + EPSILON)
    return (values * inverse, inverse)


def backward_norm(grad_normed, normed, inverse):
    return inverse * (grad_normed - normed * jnp.mean(grad_normed * normed, axis=-1, keepdims=True))


def gelu_tanh(values):
    return jax.nn.gelu(values, approximate=True)


def on_device(
    tokens,
    gain_attn,
    w_query,
    w_key,
    w_value,
    w_out,
    gain_ffn,
    w_gate,
    w_up,
    w_down,
    width_pick,
    segments,
    cotangent,
):
    level_of = width_levels(width_pick)
    peaks = (
        lax.pmax(channel_peak(w_query, 0).astype(jnp.bfloat16), ("dp", "seq")).astype(jnp.float32),
        lax.pmax(channel_peak(w_key, 0).astype(jnp.bfloat16), ("dp", "seq")).astype(jnp.float32),
        lax.pmax(channel_peak(w_value, 0).astype(jnp.bfloat16), ("dp", "seq")).astype(jnp.float32),
        lax.pmax(channel_peak(w_out, 1).astype(jnp.bfloat16), ("dp", "seq")).astype(jnp.float32),
        lax.pmax(channel_peak(w_gate, 0).astype(jnp.bfloat16), ("dp", "seq")).astype(jnp.float32),
        lax.pmax(channel_peak(w_up, 0).astype(jnp.bfloat16), ("dp", "seq")).astype(jnp.float32),
        lax.pmax(channel_peak(w_down, 1).astype(jnp.bfloat16), ("dp", "seq")).astype(jnp.float32),
    )
    peak_query, peak_key, peak_value, peak_out, peak_gate, peak_up, peak_down = peaks
    bound_query = peak_query[None, :] * level_of[0]
    bound_key = peak_key[None, :] * level_of[1]
    bound_value = peak_value[None, :] * level_of[2]
    bound_out = peak_out[:, None] * level_of[3]
    bound_gate = peak_gate[None, :] * level_of[4]
    bound_up = peak_up[None, :] * level_of[5]
    bound_down = peak_down[:, None] * level_of[6]
    fetched = (
        lax.all_gather(w_query, ("dp", "seq"), axis=0, tiled=True),
        lax.all_gather(w_key, ("dp", "seq"), axis=0, tiled=True),
        lax.all_gather(w_value, ("dp", "seq"), axis=0, tiled=True),
        lax.all_gather(gain_attn, ("dp", "seq"), axis=0, tiled=True),
        lax.all_gather(w_gate, ("dp", "seq"), axis=0, tiled=True),
        lax.all_gather(w_up, ("dp", "seq"), axis=0, tiled=True),
        lax.all_gather(gain_ffn, ("dp", "seq"), axis=0, tiled=True),
    )
    full_query, full_key, full_value, full_gain_one = (
        fetched[0],
        fetched[1],
        fetched[2],
        fetched[3],
    )
    later_rows = (fetched[4], fetched[5], fetched[6])
    columns = (
        lax.all_gather(w_out, ("dp", "seq"), axis=1, tiled=True),
        lax.all_gather(w_down, ("dp", "seq"), axis=1, tiled=True),
    )
    eff_query = bounded(full_query, bound_query)
    eff_key = bounded(full_key, bound_key)
    eff_value = bounded(full_value, bound_value)
    eff_out = bounded(columns[0], bound_out)
    eff_down = bounded(columns[1], bound_down)
    gain_one = full_gain_one.astype(jnp.float32)
    mp_count = lax.axis_size("mp")
    local_kv = HK // mp_count
    ratio = HQ // HK
    rows_here = tokens.shape[0]
    seg_row = segments[0]
    group = seg_row.shape[0]
    start = lax.axis_index("seq") * rows_here
    query_pos = start + jnp.arange(rows_here, dtype=jnp.int32)
    key_pos = jnp.arange(group, dtype=jnp.int32)
    seg_query = lax.dynamic_slice_in_dim(seg_row, start, rows_here)
    allowed = (seg_query[:, None] == seg_row[None, :]) & (key_pos[None, :] <= query_pos[:, None])
    scale = HD ** (-0.5)
    tokens_full = tokens.astype(jnp.float32)
    normed_one, inverse_one = forward_norm(tokens_full)
    hidden_one = (normed_one * gain_one).astype(jnp.bfloat16)
    query_b = jnp.dot(hidden_one, eff_query, preferred_element_type=jnp.float32).astype(
        jnp.bfloat16
    )
    key_b = jnp.dot(hidden_one, eff_key, preferred_element_type=jnp.float32).astype(jnp.bfloat16)
    value_b = jnp.dot(hidden_one, eff_value, preferred_element_type=jnp.float32).astype(
        jnp.bfloat16
    )
    key_all, value_all = (
        lax.all_gather(key_b, "seq", axis=0, tiled=True),
        lax.all_gather(value_b, "seq", axis=0, tiled=True),
    )
    query_heads = query_b.reshape(rows_here, local_kv, ratio, HD)
    key_heads = key_all.reshape(group, local_kv, HD)
    value_heads = value_all.reshape(group, local_kv, HD)

    def logits():
        raw = jnp.einsum(
            "tjrd,kjd->jrtk", query_heads, key_heads, preferred_element_type=jnp.float32
        )
        bent = jnp.tanh(raw * scale / SOFTCAP)
        capped = jnp.where(allowed[None, None], SOFTCAP * bent, -1e30)
        return (capped, bent)

    capped, bent = logits()
    largest = jnp.max(capped, axis=-1, keepdims=True)
    weights = jnp.exp(capped - largest)
    totals = jnp.sum(weights, axis=-1, keepdims=True)
    log_total = largest + jnp.log(totals)
    probs_b = (weights / totals).astype(jnp.bfloat16)
    heads_b = (
        jnp.einsum("jrtk,kjd->tjrd", probs_b, value_heads, preferred_element_type=jnp.float32)
        .reshape(rows_here, -1)
        .astype(jnp.bfloat16)
    )
    attn_total = lax.psum(jnp.dot(heads_b, eff_out, preferred_element_type=jnp.float32), "mp")
    resid = tokens_full + attn_total
    eff_gate = bounded(later_rows[0], bound_gate)
    eff_up = bounded(later_rows[1], bound_up)
    gain_two = later_rows[2].astype(jnp.float32)
    normed_two, inverse_two = forward_norm(resid)
    hidden_two = (normed_two * gain_two).astype(jnp.bfloat16)
    gate_full = jnp.dot(hidden_two, eff_gate, preferred_element_type=jnp.float32)
    upper_full = jnp.dot(hidden_two, eff_up, preferred_element_type=jnp.float32)
    gelu_value, gelu_back = jax.vjp(gelu_tanh, gate_full)
    mixed_in = (gelu_value * upper_full).astype(jnp.bfloat16)
    ffn_total = lax.psum(
        jnp.dot(mixed_in, eff_down, preferred_element_type=jnp.float32).astype(jnp.bfloat16), "mp"
    ).astype(jnp.float32)
    mixed = resid + ffn_total
    grad_mixed_in = against(cotangent, eff_down)
    grad_down_eff = inner_rows(mixed_in, cotangent)
    grad_gate_b = gelu_back(grad_mixed_in * upper_full)[0].astype(jnp.bfloat16)
    grad_upper_b = (grad_mixed_in * gelu_value).astype(jnp.bfloat16)
    grad_hidden_two = lax.psum(against(grad_gate_b, eff_gate) + against(grad_upper_b, eff_up), "mp")
    gain_two_part = jnp.sum(grad_hidden_two * normed_two, axis=0)
    grad_resid = cotangent.astype(jnp.float32) + backward_norm(
        grad_hidden_two * gain_two, normed_two, inverse_two
    )
    grad_gate_eff = inner_rows(hidden_two, grad_gate_b)
    grad_up_eff = inner_rows(hidden_two, grad_upper_b)
    grad_resid_b = grad_resid.astype(jnp.bfloat16)
    grad_heads_b = against(grad_resid_b, eff_out).astype(jnp.bfloat16)
    grad_out_eff = inner_rows(heads_b, grad_resid_b)
    grad_heads = grad_heads_b.reshape(rows_here, local_kv, ratio, HD)
    capped_again, bent_again = logits()
    probs = jnp.exp(capped_again - log_total)
    probs_again = probs.astype(jnp.bfloat16)
    grad_probs = jnp.einsum(
        "tjrd,kjd->jrtk", grad_heads, value_heads, preferred_element_type=jnp.float32
    )
    row_dot = jnp.sum(probs * grad_probs, axis=-1, keepdims=True)
    grad_raw_b = (probs * (grad_probs - row_dot) * (1.0 - bent_again * bent_again) * scale).astype(
        jnp.bfloat16
    )
    grad_query_b = (
        jnp.einsum("jrtk,kjd->tjrd", grad_raw_b, key_heads, preferred_element_type=jnp.float32)
        .reshape(rows_here, -1)
        .astype(jnp.bfloat16)
    )
    grad_key_full = jnp.einsum(
        "jrtk,tjrd->kjd", grad_raw_b, query_heads, preferred_element_type=jnp.float32
    ).reshape(group, -1)
    grad_value_full = jnp.einsum(
        "jrtk,tjrd->kjd", probs_again, grad_heads, preferred_element_type=jnp.float32
    ).reshape(group, -1)
    grad_key_sum, grad_value_sum = (
        lax.psum_scatter(grad_key_full, "seq", scatter_dimension=0, tiled=True),
        lax.psum_scatter(grad_value_full, "seq", scatter_dimension=0, tiled=True),
    )
    grad_key_b = grad_key_sum.astype(jnp.bfloat16)
    grad_value_b = grad_value_sum.astype(jnp.bfloat16)
    grad_hidden_one = lax.psum(
        against(grad_query_b, eff_query)
        + against(grad_key_b, eff_key)
        + against(grad_value_b, eff_value),
        "mp",
    )
    gain_one_part = jnp.sum(grad_hidden_one * normed_one, axis=0)
    grad_tokens = grad_resid + backward_norm(grad_hidden_one * gain_one, normed_one, inverse_one)
    grad_query_eff = inner_rows(hidden_one, grad_query_b)
    grad_key_eff = inner_rows(hidden_one, grad_key_b)
    grad_value_eff = inner_rows(hidden_one, grad_value_b)
    row_sums = (
        lax.psum_scatter(grad_query_eff, ("dp", "seq"), scatter_dimension=0, tiled=True),
        lax.psum_scatter(grad_key_eff, ("dp", "seq"), scatter_dimension=0, tiled=True),
        lax.psum_scatter(grad_value_eff, ("dp", "seq"), scatter_dimension=0, tiled=True),
        lax.psum_scatter(grad_gate_eff, ("dp", "seq"), scatter_dimension=0, tiled=True),
        lax.psum_scatter(grad_up_eff, ("dp", "seq"), scatter_dimension=0, tiled=True),
        lax.psum_scatter(gain_one_part, ("dp", "seq"), scatter_dimension=0, tiled=True),
        lax.psum_scatter(gain_two_part, ("dp", "seq"), scatter_dimension=0, tiled=True),
    )
    col_sums = (
        lax.psum_scatter(grad_out_eff, ("dp", "seq"), scatter_dimension=1, tiled=True),
        lax.psum_scatter(grad_down_eff, ("dp", "seq"), scatter_dimension=1, tiled=True),
    )
    sum_query, sum_key, sum_value, sum_gate, sum_up, sum_gain_one, sum_gain_two = row_sums
    out_sum, sum_down = col_sums
    grad_query = sum_query * bound_slope(w_query, bound_query)
    grad_key = sum_key * bound_slope(w_key, bound_key)
    grad_value = sum_value * bound_slope(w_value, bound_value)
    grad_gate = sum_gate * bound_slope(w_gate, bound_gate)
    grad_up = sum_up * bound_slope(w_up, bound_up)
    grad_out = out_sum * bound_slope(w_out, bound_out)
    grad_down = sum_down * bound_slope(w_down, bound_down)
    attn_scales = jnp.stack([peak_query, peak_out])
    kv_scales = jnp.stack([peak_key, peak_value])
    ffn_scales = jnp.stack([peak_gate, peak_up, peak_down])
    return (
        mixed,
        grad_tokens,
        grad_query,
        grad_key,
        grad_value,
        grad_out,
        grad_gate,
        grad_up,
        grad_down,
        sum_gain_one,
        sum_gain_two,
        attn_scales,
        kv_scales,
        ffn_scales,
    )


def solution(mesh):
    in_specs = (
        P(("dp", "seq"), None),
        P(("dp", "seq")),
        P(("dp", "seq"), "mp"),
        P(("dp", "seq"), "mp"),
        P(("dp", "seq"), "mp"),
        P("mp", ("dp", "seq")),
        P(("dp", "seq")),
        P(("dp", "seq"), "mp"),
        P(("dp", "seq"), "mp"),
        P("mp", ("dp", "seq")),
        P(),
        P("dp", None),
        P(("dp", "seq"), None),
    )
    out_specs = (
        P(("dp", "seq"), None),
        P(("dp", "seq"), None),
        P(("dp", "seq"), "mp"),
        P(("dp", "seq"), "mp"),
        P(("dp", "seq"), "mp"),
        P("mp", ("dp", "seq")),
        P(("dp", "seq"), "mp"),
        P(("dp", "seq"), "mp"),
        P("mp", ("dp", "seq")),
        P(("dp", "seq")),
        P(("dp", "seq")),
        P(None, "mp"),
        P(None, "mp"),
        P(None, "mp"),
    )
    return jax.shard_map(
        on_device, mesh=mesh, in_specs=in_specs, out_specs=out_specs, check_vma=False
    )
```

profile of v0, /device:TPU:0, one launch (start us, length us, event | category | flops | bytes accessed | tf_op | source)
XLA Modules:
  0.0 1682.0 jit_solution(11624770434214591259)
XLA Ops:
  20.9 25.8 %all-reduce.6 = (bf16[512]{0:T(512)(128)(2,1)S(1)}, bf16[256]{0:T(256)(128)(2,1)S(1)}, bf16[256]{0:T(256)(128)(2,1)S(1)}, bf16[512]{0:T(512)(128)(2,1)S(1)}, bf1...) all-reduce(bf16[512]{0:T(512)(128)(2,1)S(1)} %fusion.66, ...), channel_id=1, replica_groups=mesh['dp'=4,'seq'=2,'mp'=4] {'dp','seq'}, use_global_device_ids=true, to_apply=%region_6.7 | all-reduce | flops 8448 | bytes 33792 | tf_op jit(solution)/shard_map/pmax | solution.py:76
  51.8 22.7 %all-reduce.5 = (bf16[2304]{0:T(1024)(128)(2,1)S(1)}, bf16[2304]{0:T(1024)(128)(2,1)S(1)}) all-reduce(bf16[2304]{0:T(1024)(128)(2,1)S(1)} %dynamic-update-slice, bf16[2304]{0:T(1024)(128)(2,1)S(1)} %dynamic-update-slice.1), channel_id=1, replica_groups=mesh['dp'=4,'seq'=2,'mp'=4] {'dp','seq'}, use_global_device_ids=true, to_apply=%add | all-reduce | flops 4608 | bytes 18432
  76.7 9.0 all_gather.37
  88.2 9.9 all_gather.35
  106.5 19.0 %all-gather.14.cloned.1.call-done = bf16[512,2304]{0,1:T(8,128)(2,1)} async-done(((bf16[512,288]{0,1:T(8,128)(2,1)}), bf16[512,2304]{0,1:T(8,128)(2,1)}) %all-gather.14.cloned.1.call-update) | async-done | bytes 2359312 | tf_op jit(solution)/shard_map/all_gather | solution.py:109
  135.6 167.4 %all-reduce.12.cloned.1.call-done = f32[512,2304]{1,0:T(8,128)} async-done(((f32[512,2304]{1,0:T(8,128)}), f32[512,2304]{1,0:T(8,128)}) %all-reduce.12.cloned.1.call-update) | async-done | bytes 4718608 | tf_op jit(solution)/shard_map/psum | solution.py:167
  308.7 58.9 %all-gather.18.cloned.1.call-done = bf16[2304,2304]{1,0:T(8,128)(2,1)} async-done(((bf16[288,2304]{1,0:T(8,128)(2,1)}), bf16[2304,2304]{1,0:T(8,128)(2,1)}) %all-gather.18.cloned.1.call-update) | async-done | bytes 10616848 | tf_op jit(solution)/shard_map/all_gather | solution.py:98
  367.6 6.9 multiply_convert_fusion.1
  379.4 7.3 fusion.116
  386.6 46.7 %all-gather.16.cloned.1.call-done = bf16[2304,2304]{1,0:T(8,128)(2,1)} async-done(((bf16[288,2304]{1,0:T(8,128)(2,1)}), bf16[2304,2304]{1,0:T(8,128)(2,1)}) %all-gather.16.cloned.1.call-update) | async-done | bytes 10616848 | tf_op jit(solution)/shard_map/all_gather | solution.py:97
  445.1 7.3 fusion.115
  452.4 46.6 %all-gather.20.cloned.1.call-done = bf16[2304,2304]{0,1:T(8,128)(2,1)} async-done(((bf16[2304,288]{0,1:T(8,128)(2,1)}), bf16[2304,2304]{0,1:T(8,128)(2,1)}) %all-gather.20.cloned.1.call-update) | async-done | bytes 10616848 | tf_op jit(solution)/shard_map/all_gather | solution.py:110
  506.0 16.4 multiply_convert_fusion.3
  522.4 12.0 fusion.117
  534.5 9.4 convolution_add_fusion.2
  544.0 11.3 convolution_convert_fusion
  555.4 160.6 %all-reduce.16.cloned.1.call-done = f32[512,2304]{1,0:T(8,128)} async-done(((f32[512,2304]{1,0:T(8,128)}), f32[512,2304]{1,0:T(8,128)}) %all-reduce.16.cloned.1.call-update) | async-done | bytes 4718608 | tf_op jit(solution)/shard_map/psum | solution.py:186
  720.9 92.6 %all-reduce.14.cloned.1.call-done = bf16[512,2304]{1,0:T(8,128)(2,1)} async-done(((bf16[512,2304]{1,0:T(8,128)(2,1)}), bf16[512,2304]{1,0:T(8,128)(2,1)}) %all-reduce.14.cloned.1.call-update) | async-done | bytes 2359312 | tf_op jit(solution)/shard_map/psum | solution.py:178
  836.7 9.9 reduce-scatter.12.cloned.1.call-done
  850.2 18.9 %reduce-scatter.10.cloned.1.call-done = f32[512,256]{0,1:T(8,128)} async-done(((f32[1024,256]{0,1:T(8,128)}), f32[512,256]{0,1:T(8,128)}) %reduce-scatter.10.cloned.1.call-update) | async-done | bytes 524304 | tf_op jit(solution)/shard_map/reduce_scatter | solution.py:219
  894.3 12.2 fusion.120
  906.6 12.1 fusion.119
  918.8 12.8 fusion.118
  936.5 24.6 %reduce-scatter.16.cloned.1.call-done = f32[288,256]{1,0:T(8,128)} async-done(((f32[2304,256]{1,0:T(8,128)}), f32[288,256]{1,0:T(8,128)}) %reduce-scatter.16.cloned.1.call-update) | async-done | bytes 294928 | tf_op jit(solution)/shard_map/reduce_scatter | solution.py:237
  962.8 172.4 %all-reduce.18.cloned.1.call-done = f32[512,2304]{1,0:T(8,128)} async-done(((f32[512,2304]{1,0:T(8,128)}), f32[512,2304]{1,0:T(8,128)}) %all-reduce.18.cloned.1.call-update) | async-done | bytes 4718608 | tf_op jit(solution)/shard_map/psum | solution.py:224
  1138.8 24.6 %all-reduce.4 = (f32[2304]{0:T(1024)S(1)}, f32[2304]{0:T(1024)S(1)}) all-reduce(f32[2304]{0:T(1024)S(1)} %get-tuple-element.16, f32[2304]{0:T(1024)S(1)} %get-tuple-element.14), channel_id=11, replica_groups=mesh['dp'=4,'seq'=2,'mp'=4] {'dp','seq'}, use_global_device_ids=true, to_apply=%region_35.36.clone | all-reduce | flops 4608 | bytes 36864
  1164.7 7.3 fusion.15
  1172.0 19.4 %reduce-scatter.20.cloned.1.call-done = f32[512,288]{0,1:T(8,128)} async-done(((f32[512,2304]{0,1:T(8,128)}), f32[512,288]{0,1:T(8,128)}) %reduce-scatter.20.cloned.1.call-update) | async-done | bytes 589840 | tf_op jit(solution)/shard_map/reduce_scatter | solution.py:245
  1193.5 55.6 %reduce-scatter.14.cloned.1.call-done = f32[288,512]{1,0:T(8,128)} async-done(((f32[2304,512]{1,0:T(8,128)}), f32[288,512]{1,0:T(8,128)}) %reduce-scatter.14.cloned.1.call-update) | async-done | bytes 589840 | tf_op jit(solution)/shard_map/reduce_scatter | solution.py:236
  1251.1 138.7 %reduce-scatter.26.cloned.1.call-done = f32[2304,288]{0,1:T(8,128)} async-done(((f32[2304,2304]{0,1:T(8,128)}), f32[2304,288]{0,1:T(8,128)}) %reduce-scatter.26.cloned.1.call-update) | async-done | bytes 2654224 | tf_op jit(solution)/shard_map/reduce_scatter | solution.py:246
  1393.9 136.7 %reduce-scatter.24.cloned.1.call-done = f32[288,2304]{1,0:T(8,128)} async-done(((f32[2304,2304]{1,0:T(8,128)}), f32[288,2304]{1,0:T(8,128)}) %reduce-scatter.24.cloned.1.call-update) | async-done | bytes 2654224 | tf_op jit(solution)/shard_map/reduce_scatter | solution.py:240
  1534.3 136.9 %reduce-scatter.22.cloned.1.call-done = f32[288,2304]{1,0:T(8,128)} async-done(((f32[2304,2304]{1,0:T(8,128)}), f32[288,2304]{1,0:T(8,128)}) %reduce-scatter.22.cloned.1.call-update) | async-done | bytes 2654224 | tf_op jit(solution)/shard_map/reduce_scatter | solution.py:239
  (269 shorter events, 153.5 us)
Async XLA Ops:
  7.2 67.2 %all-gather.10.cloned.1.call-start = ((), (), s32[]{:S(2)}) async-start(), calls=%async_computation.10 | async-start | bytes 1327104 | tf_op jit(solution)/shard_map/all_gather | solution.py:94
  7.9 77.8 %all-gather.8.cloned.1.call-start = ((), (), s32[]{:S(2)}) async-start(), calls=%async_computation.9 | async-start | bytes 1327104 | tf_op jit(solution)/shard_map/all_gather | solution.py:95
  8.7 89.4 %all-gather.12.cloned.1.call-start = ((), (), s32[]{:S(2)}) async-start(), calls=%async_computation.11 | async-start | bytes 2654208 | tf_op jit(solution)/shard_map/all_gather | solution.py:93
  9.5 116.1 %all-gather.14.cloned.1.call-start = ((), (), s32[]{:S(2)}) async-start(), calls=%async_computation.12 | async-start | bytes 2654208 | tf_op jit(solution)/shard_map/all_gather | solution.py:109
  10.0 293.0 %all-reduce.12.cloned.1.call-start = ((), (), s32[]{:S(2)}) async-start(), calls=%async_computation.13 | async-start | bytes 9437184 | tf_op jit(solution)/shard_map/psum | solution.py:167
  46.7 86.8 %copy-start.42 = (bf16[2304]{0:T(1024)(128)(2,1)}, bf16[2304]{0:T(1024)(128)(2,1)S(1)}, u32[]{:S(2)}) copy-start(bf16[2304]{0:T(1024)(128)(2,1)S(1)} %get-tuple-element.26) | copy-start | bytes 13828
  46.7 87.5 %copy-start.40 = (bf16[2304]{0:T(1024)(128)(2,1)}, bf16[2304]{0:T(1024)(128)(2,1)S(1)}, u32[]{:S(2)}) copy-start(bf16[2304]{0:T(1024)(128)(2,1)S(1)} %get-tuple-element.27) | copy-start | bytes 13828
  46.7 88.2 %copy-start.38 = (bf16[2304]{0:T(1024)(128)(2,1)}, bf16[2304]{0:T(1024)(128)(2,1)S(1)}, u32[]{:S(2)}) copy-start(bf16[2304]{0:T(1024)(128)(2,1)S(1)} %get-tuple-element.28) | copy-start | bytes 13828
  130.9 236.7 %all-gather.18.cloned.1.call-start = ((), (), s32[]{:S(2)}) async-start(), calls=%async_computation.15 | async-start | bytes 11943936 | tf_op jit(solution)/shard_map/all_gather | solution.py:98
  131.5 301.8 %all-gather.16.cloned.1.call-start = ((), (), s32[]{:S(2)}) async-start(), calls=%async_computation.14 | async-start | bytes 11943936 | tf_op jit(solution)/shard_map/all_gather | solution.py:97
  132.2 366.8 %all-gather.20.cloned.1.call-start = ((), (), s32[]{:S(2)}) async-start(), calls=%async_computation.16 | async-start | bytes 11943936 | tf_op jit(solution)/shard_map/all_gather | solution.py:110
  133.0 583.0 %all-reduce.16.cloned.1.call-start = ((), (), s32[]{:S(2)}) async-start(), calls=%async_computation.18 | async-start | bytes 9437184 | tf_op jit(solution)/shard_map/psum | solution.py:186
  134.2 233.4 %copy-start.32 = (f32[2304]{0:T(1024)}, f32[2304]{0:T(1024)S(1)}, u32[]{:S(2)}) copy-start(f32[2304]{0:T(1024)S(1)} %broadcast_multiply_fusion.1) | copy-start | bytes 27652
  134.9 298.4 %copy-start.30 = (f32[2304]{0:T(1024)}, f32[2304]{0:T(1024)S(1)}, u32[]{:S(2)}) copy-start(f32[2304]{0:T(1024)S(1)} %broadcast_multiply_fusion.2) | copy-start | bytes 27652
  135.6 363.4 %copy-start.34 = (f32[2304]{0:T(1024)}, f32[2304]{0:T(1024)S(1)}, u32[]{:S(2)}) copy-start(f32[2304]{0:T(1024)S(1)} %broadcast_multiply_fusion) | copy-start | bytes 27652
  308.7 131.5 %copy-start.19 = (bf16[512,2304]{1,0:T(8,128)(2,1)}, bf16[512,2304]{1,0:T(8,128)(2,1)S(1)}, u32[]{:S(2)}) copy-start(bf16[512,2304]{1,0:T(8,128)(2,1)S(1)} %multiply_convert_fusion.5) | copy-start | bytes 7077892
  543.9 269.6 %all-reduce.14.cloned.1.call-start = ((), (), s32[]{:S(2)}) async-start(), calls=%async_computation.17 | async-start | bytes 4718592 | tf_op jit(solution)/shard_map/psum | solution.py:178
  555.3 291.3 %reduce-scatter.12.cloned.1.call-start = ((), (), s32[]{:S(2)}) async-start(), calls=%async_computation.20 | async-start | bytes 1572864 | tf_op jit(solution)/shard_map/reduce_scatter | solution.py:220
  827.1 42.0 %reduce-scatter.10.cloned.1.call-start = ((), (), s32[]{:S(2)}) async-start(), calls=%async_computation.19 | async-start | bytes 1572864 | tf_op jit(solution)/shard_map/reduce_scatter | solution.py:219
  836.7 98.1 %reduce-scatter.18.cloned.1.call-start = ((), (), s32[]{:S(2)}) async-start(), calls=%async_computation.24 | async-start | bytes 2654208 | tf_op jit(solution)/shard_map/reduce_scatter | solution.py:238
  850.1 110.9 %reduce-scatter.16.cloned.1.call-start = ((), (), s32[]{:S(2)}) async-start(), calls=%async_computation.23 | async-start | bytes 2654208 | tf_op jit(solution)/shard_map/reduce_scatter | solution.py:237
  872.6 262.7 %all-reduce.18.cloned.1.call-start = ((), (), s32[]{:S(2)}) async-start(), calls=%async_computation.21 | async-start | bytes 9437184 | tf_op jit(solution)/shard_map/psum | solution.py:224
  882.2 309.3 %reduce-scatter.20.cloned.1.call-start = ((), (), s32[]{:S(2)}) async-start(), calls=%async_computation.25 | async-start | bytes 5308416 | tf_op jit(solution)/shard_map/reduce_scatter | solution.py:245
  889.4 359.7 %reduce-scatter.14.cloned.1.call-start = ((), (), s32[]{:S(2)}) async-start(), calls=%async_computation.22 | async-start | bytes 5308416 | tf_op jit(solution)/shard_map/reduce_scatter | solution.py:236
  894.2 495.5 %reduce-scatter.26.cloned.1.call-start = ((), (), s32[]{:S(2)}) async-start(), calls=%async_computation.28 | async-start | bytes 23887872 | tf_op jit(solution)/shard_map/reduce_scatter | solution.py:246
  906.5 624.0 %reduce-scatter.24.cloned.1.call-start = ((), (), s32[]{:S(2)}) async-start(), calls=%async_computation.27 | async-start | bytes 23887872 | tf_op jit(solution)/shard_map/reduce_scatter | solution.py:240
  918.7 752.5 %reduce-scatter.22.cloned.1.call-start = ((), (), s32[]{:S(2)}) async-start(), calls=%async_computation.26 | async-start | bytes 23887872 | tf_op jit(solution)/shard_map/reduce_scatter | solution.py:239
  1164.7 225.0 %copy-start.35 = (f32[2304]{0:T(1024)S(1)}, f32[2304]{0:T(1024)}, u32[]{:S(2)}) copy-start(f32[2304]{0:T(1024)} %copy-done.34) | copy-start | bytes 27652
  1193.5 337.1 %copy-start.8 = (bf16[288,2304]{1,0:T(8,128)(2,1)S(1)}, bf16[288,2304]{1,0:T(8,128)(2,1)}, u32[]{:S(2)}) copy-start(bf16[288,2304]{1,0:T(8,128)(2,1)} %param.21) | copy-start | bytes 3981316
  1193.5 337.1 %copy-start.33 = (f32[2304]{0:T(1024)S(1)}, f32[2304]{0:T(1024)}, u32[]{:S(2)}) copy-start(f32[2304]{0:T(1024)} %copy-done.32) | copy-start | bytes 27652
  1393.9 277.3 %copy-start.9 = (bf16[288,2304]{1,0:T(8,128)(2,1)S(1)}, bf16[288,2304]{1,0:T(8,128)(2,1)}, u32[]{:S(2)}) copy-start(bf16[288,2304]{1,0:T(8,128)(2,1)} %param.20) | copy-start | bytes 3981316
  1393.9 277.3 %copy-start.31 = (f32[2304]{0:T(1024)S(1)}, f32[2304]{0:T(1024)}, u32[]{:S(2)}) copy-start(f32[2304]{0:T(1024)} %copy-done.30) | copy-start | bytes 27652
  (61 other events, 969.9 us)
Sparse Core Ops, SparseCore 0:
  9.9 26.9 all-gather.9
  38.8 24.2 all-gather.7
  64.9 30.0 all-gather.11
  96.8 28.7 all-gather.13
  131.0 171.9 all-reduce.11
  304.7 62.7 all-gather.17
  369.5 63.7 all-gather.15
  435.2 63.7 all-gather.19
  544.0 171.9 all-reduce.15
  718.8 94.6 all-reduce.13
  827.2 19.3 reduce-scatter.11
  848.7 20.3 reduce-scatter.9
  872.4 42.4 reduce-scatter.17
  918.5 42.4 reduce-scatter.15
  963.3 171.9 all-reduce.17
  1138.6 52.8 reduce-scatter.19
  1195.2 53.8 reduce-scatter.13
  1252.5 137.1 reduce-scatter.25
  1393.4 137.1 reduce-scatter.23
  1534.0 137.1 reduce-scatter.21
where the time goes:
time: 1690 us; the launch traced here: 1680 us
  waiting for transfers between devices  1310 us (78%)
  matrix products  154 us (9%)
  blocking collectives  91.9 us (5%)
  other arithmetic  86.4 us (5%)
  local copies, waits for them, and re-layouts  21.8 us (1%)
    psum x1, waiting for transfers between devices, on_device(): lax.psum(against(grad_query_b, eff_query) + against(grad_key_b, eff_key)...  172 us
    psum x1, waiting for transfers between devices, on_device(): lax.psum(jnp.dot(heads_b, eff_out, preferred_element_type=jnp.float32), '...  167 us
    psum x1, waiting for transfers between devices, on_device(): lax.psum(against(grad_gate_b, eff_gate) + against(grad_upper_b, eff_up),...  161 us
    reduce_scatter x1, waiting for transfers between devices, on_device(): lax.psum_scatter(grad_down_eff, ('dp', 'seq'), scatter_dimension=1, tiled...  139 us
    reduce_scatter x1, waiting for transfers between devices, on_device(): lax.psum_scatter(grad_gate_eff, ('dp', 'seq'), scatter_dimension=0, tiled...  137 us
    reduce_scatter x1, waiting for transfers between devices, on_device(): lax.psum_scatter(grad_up_eff, ('dp', 'seq'), scatter_dimension=0, tiled=T...  137 us
    psum x1, waiting for transfers between devices, on_device(): lax.psum(jnp.dot(mixed_in, eff_down, preferred_element_type=jnp.float32)....  92.6 us
    all_gather x1, waiting for transfers between devices, on_device(): lax.all_gather(w_up, ('dp', 'seq'), axis=0, tiled=True)  58.9 us
  transfers between devices with their start and end apart: 20, of which 16 were waited for; matrix products, arithmetic and copies ran while one was open for 11% of the time, Pallas kernels for 0%

commit v1 on v0

--- a/solution.py
+++ b/solution.py
@@ -275,6 +275,369 @@
     )
 
 
+F32 = jnp.float32
+BF16 = jnp.bfloat16
+
+
+def over_x(values):
+    return lax.ppermute(values, "dp", [(i, i ^ 2) for i in range(4)])
+
+
+def over_core(values):
+    return lax.ppermute(values, "dp", [(i, i ^ 1) for i in range(4)])
+
+
+def over_y(values):
+    return lax.ppermute(values, "seq", [(0, 1), (1, 0)])
+
+
+def over_z(values, step):
+    return lax.ppermute(values, "mp", [(i, i ^ step) for i in range(4)])
+
+
+def after(values, *others):
+    return lax.optimization_barrier((values,) + others)[0]
+
+
+def natural(left, right):
+    return jnp.dot(left, right, preferred_element_type=F32)
+
+
+def half_of(values, index, axis):
+    size = values.shape[axis] // 2
+    return lax.dynamic_slice_in_dim(values, index * size, size, axis)
+
+
+def placed(parts, x, y):
+    own, from_x, from_y, from_xy = parts
+    blank = jnp.zeros((2, own.shape[0], 2) + own.shape[1:], own.dtype)
+
+    def put(into, part, i, j):
+        at = (i, 0, j) + (0,) * (own.ndim - 1)
+        return lax.dynamic_update_slice(into, part[None, :, None], at)
+
+    full = put(blank, own, x, y)
+    full = put(full, from_x, 1 - x, y)
+    full = put(full, from_y, x, 1 - y)
+    return put(full, from_xy, 1 - x, 1 - y)
+
+
+def z_chunk(values, index):
+    size = values.shape[0] // 4
+    return lax.dynamic_slice_in_dim(values, index * size, size, 0)
+
+
+def z_scatter(partial, z):
+    partial_b = partial.astype(BF16)
+    arrived = [over_z(z_chunk(partial_b, z ^ step), step) for step in (2, 3, 1)]
+    total = z_chunk(partial, z)
+    for part in arrived:
+        total = total + part.astype(F32)
+    return total
+
+
+def z_gather(chunk, z):
+    size = chunk.shape[0]
+    full = jnp.zeros((4 * size,) + chunk.shape[1:], chunk.dtype)
+    full = lax.dynamic_update_slice_in_dim(full, chunk, z * size, 0)
+    for step in (2, 3, 1):
+        part = over_z(chunk, step)
+        full = lax.dynamic_update_slice_in_dim(full, part, (z ^ step) * size, 0)
+    return full
+
+
+def paired_block(
+    tokens,
+    gain_attn,
+    w_query,
+    w_key,
+    w_value,
+    w_out,
+    gain_ffn,
+    w_gate,
+    w_up,
+    w_down,
+    width_pick,
+    segments,
+    cotangent,
+):
+    dp, y, z = lax.axis_index("dp"), lax.axis_index("seq"), lax.axis_index("mp")
+    x, core = dp // 2, dp % 2
+    rows, width = tokens.shape
+    share = w_query.shape[0]
+    n_query, n_key, hidden = w_query.shape[1], w_key.shape[1], w_gate.shape[1]
+    half = hidden // 2
+    level_of = width_levels(width_pick)
+
+    down_t = w_down.T
+    w_ffn = (w_down.T, w_gate, w_up)
+    raw = [jnp.stack([half_of(w, core, 1), over_core(half_of(w, 1 - core, 1))]) for w in w_ffn]
+    cot_other = over_core(cotangent)
+
+    sizes = [n_query, n_key, n_key, n_query, hidden, hidden, hidden]
+    peaks = jnp.concatenate(
+        [
+            jnp.max(jnp.abs(w), axis=axis)
+            for w, axis in (
+                (w_query, 0),
+                (w_key, 0),
+                (w_value, 0),
+                (w_out, 1),
+                (w_gate, 0),
+                (w_up, 0),
+                (w_down, 1),
+            )
+        ]
+    )
+    place = ((x * 2 + core) * 2 + y) * share
+    gains = jnp.zeros((2, width), BF16)
+    gains = lax.dynamic_update_slice(gains, jnp.stack([gain_attn, gain_ffn]), (0, place))
+    small = (peaks, gains)
+    for send in (over_core, over_x, over_y):
+        got = send(jnp.concatenate([small[0], small[1].reshape(-1)]))
+        small = (
+            jnp.maximum(small[0], got[: peaks.size]),
+            small[1] + got[peaks.size :].reshape(2, width),
+        )
+    gain_one, gain_two = small[1][0].astype(F32), small[1][1].astype(F32)
+    peak, at = [], 0
+    for size in sizes:
+        peak.append(small[0][at : at + size].astype(F32))
+        at += size
+    bounds = [p * level_of[i] for i, p in enumerate(peak)]
+    b_query, b_key, b_value, b_out, b_gate, b_up, b_down = bounds
+
+    e_attn = jnp.concatenate(
+        [
+            bounded(w_query, b_query[None, :]),
+            bounded(w_key, b_key[None, :]),
+            bounded(w_value, b_value[None, :]),
+            bounded(w_out, b_out[:, None]).T,
+        ],
+        axis=1,
+    )
+    attn_x, attn_y, attn_core = over_x(e_attn), over_y(e_attn), over_core(e_attn)
+    mid = e_attn.shape[1] // 2
+    attn_xy = jnp.concatenate([over_y(attn_x[:, :mid]), over_x(attn_y[:, mid:])], axis=1)
+    core_x, core_y, core_xy = over_core(attn_x), over_core(attn_y), over_core(attn_xy)
+
+    def both(mine, theirs):
+        pair = jnp.stack([mine, theirs])
+        return jnp.where(core == 0, pair, pair[::-1])
+
+    e_attn_full = placed(
+        (
+            both(e_attn, attn_core),
+            both(attn_x, core_x),
+            both(attn_y, core_y),
+            both(attn_xy, core_xy),
+        ),
+        x,
+        y,
+    ).reshape(width, -1)
+    n_in = n_query + 2 * n_key
+    e_in, e_out_t = e_attn_full[:, :n_in], e_attn_full[:, n_in:]
+
+    def gathered(raw_pair, bound, earlier):
+        mine = bounded(raw_pair, half_of(bound, core, 0)[None, None, :])
+        mine = jnp.where(core == 0, mine, mine[::-1])
+        mine = after(mine, earlier)
+        from_x, from_y = over_x(mine), over_y(mine)
+        first, second = over_y(from_x[0]), over_x(from_y[1])
+        diagonal = jnp.stack([first, second])
+        return placed((mine, from_x, from_y, diagonal), x, y).reshape(width, half), from_x
+
+    e_down_t, mark = gathered(raw[0], b_down, attn_x)
+    e_gate, mark = gathered(raw[1], b_gate, mark)
+    e_up, mark = gathered(raw[2], b_up, mark)
+
+    tokens_full = tokens.astype(F32)
+    normed_one, _ = forward_norm(tokens_full)
+    hidden_one = (normed_one * gain_one).astype(BF16)
+    projected = natural(hidden_one, e_in).astype(BF16)
+    query_b = projected[:, :n_query]
+    kv_own = projected[:, n_query:]
+    kv_other = over_y(kv_own)
+    kv = jnp.concatenate([kv_own, kv_other], axis=0)
+    ratio = n_query // HD
+    query_heads = query_b.reshape(rows, ratio, HD)
+    key_all, value_all = kv[:, :HD], kv[:, HD:]
+    seg_row = segments[0]
+    own_at, other_at = y * rows, (1 - y) * rows
+    order = jnp.arange(rows, dtype=jnp.int32)
+    query_pos = own_at + order
+    key_pos = jnp.concatenate([own_at + order, other_at + order])
+    seg_query = lax.dynamic_slice_in_dim(seg_row, own_at, rows)
+    seg_key = jnp.concatenate([seg_query, lax.dynamic_slice_in_dim(seg_row, other_at, rows)])
+    allowed = (seg_query[:, None] == seg_key[None, :]) & (key_pos[None, :] <= query_pos[:, None])
+    scale = HD ** (-0.5)
+
+    def logits():
+        raw = jnp.einsum("trd,kd->rtk", query_heads, key_all, preferred_element_type=F32)
+        bent = jnp.tanh(raw * scale / SOFTCAP)
+        capped = jnp.where(allowed[None], SOFTCAP * bent, -1e30)
+        return capped, bent
+
+    capped, bent = logits()
+    largest = jnp.max(capped, axis=-1, keepdims=True)
+    weights = jnp.exp(capped - largest)
+    totals = jnp.sum(weights, axis=-1, keepdims=True)
+    log_total = largest + jnp.log(totals)
+    probs_b = (weights / totals).astype(BF16)
+    heads_b = (
+        jnp.einsum("rtk,kd->trd", probs_b, value_all, preferred_element_type=F32)
+        .reshape(rows, -1)
+        .astype(BF16)
+    )
+    attn_chunk = z_scatter(against(heads_b, e_out_t), z)
+
+    resid = z_chunk(tokens, z).astype(F32) + attn_chunk
+    normed_two, inverse_two = forward_norm(resid)
+    hidden_two = z_gather((normed_two * gain_two).astype(BF16), z)
+    hidden_two = jnp.concatenate([hidden_two, over_core(hidden_two)], axis=0)
+    cot_pair = jnp.concatenate([cotangent, cot_other], axis=0)
+    grad_mixed_in = natural(cot_pair, e_down_t)
+    gate_full = natural(hidden_two, e_gate)
+    upper_full = natural(hidden_two, e_up)
+    gelu_value, gelu_back = jax.vjp(gelu_tanh, gate_full)
+    mixed_in = (gelu_value * upper_full).astype(BF16)
+    grad_gate_b = gelu_back(grad_mixed_in * upper_full)[0].astype(BF16)
+    grad_upper_b = (grad_mixed_in * gelu_value).astype(BF16)
+    back_part = against(grad_gate_b, e_gate) + against(grad_upper_b, e_up)
+    back_part = back_part[:rows] + over_core(back_part[rows:].astype(BF16)).astype(F32)
+    grad_hidden_two = z_scatter(back_part, z)
+    gain_two_part = jnp.sum(grad_hidden_two * normed_two, axis=0)
+    grad_resid = z_chunk(cotangent, z).astype(F32) + backward_norm(
+        grad_hidden_two * gain_two, normed_two, inverse_two
+    )
+    grad_resid_b = z_gather(grad_resid.astype(BF16), z)
+
+    def scattered(left, right):
+        grad = inner_rows(left, right).astype(BF16).reshape(2, 2, 2, share, half)
+
+        def pick(values, index, axis):
+            return lax.dynamic_index_in_dim(values, index, axis, keepdims=False)
+
+        first, second = grad[:, 0], grad[:, 1]
+        first = pick(first, x, 0).astype(F32) + over_x(pick(first, 1 - x, 0)).astype(F32)
+        second = pick(second, y, 1).astype(F32) + over_y(pick(second, 1 - y, 1)).astype(F32)
+        first = pick(first, y, 0) + over_y(pick(first, 1 - y, 0).astype(BF16)).astype(F32)
+        second = pick(second, x, 0) + over_x(pick(second, 1 - x, 0).astype(BF16)).astype(F32)
+        mine = jnp.where(core == 0, first, second)
+        theirs = over_core(jnp.where(core == 0, second, first).astype(BF16)).astype(F32)
+        return jnp.where(
+            core == 0,
+            jnp.concatenate([mine, theirs], axis=1),
+            jnp.concatenate([theirs, mine], axis=1),
+        )
+
+    sum_gate = scattered(hidden_two, grad_gate_b)
+    sum_up = scattered(hidden_two, grad_upper_b)
+    sum_down = scattered(cot_pair, mixed_in).T
+
+    ffn_part = against(mixed_in, e_down_t)
+    ffn_part = ffn_part[:rows] + over_core(ffn_part[rows:].astype(BF16)).astype(F32)
+    mixed = z_gather((resid + z_scatter(ffn_part, z)).astype(BF16), z).astype(F32)
+
+    grad_heads = natural(grad_resid_b, e_out_t).astype(BF16).reshape(rows, ratio, HD)
+    capped_again, bent_again = logits()
+    probs = jnp.exp(capped_again - log_total)
+    probs_again = probs.astype(BF16)
+    grad_probs = jnp.einsum("trd,kd->rtk", grad_heads, value_all, preferred_element_type=F32)
+    row_dot = jnp.sum(probs * grad_probs, axis=-1, keepdims=True)
+    grad_raw_b = (probs * (grad_probs - row_dot) * (1.0 - bent_again * bent_again) * scale).astype(
+        BF16
+    )
+    grad_query_b = (
+        jnp.einsum("rtk,kd->trd", grad_raw_b, key_all, preferred_element_type=F32)
+        .reshape(rows, -1)
+        .astype(BF16)
+    )
+    grad_kv = jnp.concatenate(
+        [
+            jnp.einsum("rtk,trd->kd", grad_raw_b, query_heads, preferred_element_type=F32),
+            jnp.einsum("rtk,trd->kd", probs_again, grad_heads, preferred_element_type=F32),
+        ],
+        axis=1,
+    )
+    grad_kv_b = (grad_kv[:rows] + over_y(grad_kv[rows:].astype(BF16)).astype(F32)).astype(BF16)
+    grad_in_b = jnp.concatenate([grad_query_b, grad_kv_b], axis=1)
+    grad_hidden_one = z_scatter(against(grad_in_b, e_in), z)
+    chunk_one, inverse_one = forward_norm(z_chunk(tokens, z).astype(F32))
+    gain_one_part = jnp.sum(grad_hidden_one * chunk_one, axis=0)
+    grad_chunk = grad_resid + backward_norm(grad_hidden_one * gain_one, chunk_one, inverse_one)
+    grad_tokens = z_gather(grad_chunk.astype(BF16), z).astype(F32)
+
+    def core_rows(values):
+        return lax.dynamic_index_in_dim(
+            values.reshape(values.shape[0], 2, 2, 2 * share), core, 2, keepdims=False
+        ).reshape(values.shape[0], -1)
+
+    def core_pair(values):
+        pair = values.reshape(values.shape[0], 2, 2, 2 * share)
+        mine = lax.dynamic_index_in_dim(pair, core, 2, keepdims=False)
+        theirs = lax.dynamic_index_in_dim(pair, 1 - core, 2, keepdims=False)
+        return jnp.concatenate([mine, over_core(theirs)], axis=0).reshape(2 * rows, -1)
+
+    hidden_pair = core_pair(hidden_one)
+    resid_pair = core_pair(grad_resid_b)
+    heads_pair = jnp.concatenate([heads_b, over_core(heads_b)], axis=0)
+    in_pair = jnp.concatenate([grad_in_b, over_core(grad_in_b)], axis=0)
+
+    def scattered_rows(left, right):
+        grad = inner_rows(left, right).astype(BF16)
+        cut = grad.shape[1] // 2
+        grad = grad.reshape(2, 2, share, -1)
+
+        def pick(values, index, axis):
+            return lax.dynamic_index_in_dim(values, index, axis, keepdims=False)
+
+        first, second = grad[..., :cut], grad[..., cut:]
+        first = pick(first, x, 0).astype(F32) + over_x(pick(first, 1 - x, 0)).astype(F32)
+        second = pick(second, y, 1).astype(F32) + over_y(pick(second, 1 - y, 1)).astype(F32)
+        first = pick(first, y, 0) + over_y(pick(first, 1 - y, 0).astype(BF16)).astype(F32)
+        second = pick(second, x, 0) + over_x(pick(second, 1 - x, 0).astype(BF16)).astype(F32)
+        return jnp.concatenate([first, second], axis=1)
+
+    sum_out = scattered_rows(resid_pair, heads_pair).T
+    sum_in = scattered_rows(hidden_pair, in_pair)
+    sum_query = sum_in[:, :n_query]
+    sum_key = sum_in[:, n_query : n_query + n_key]
+    sum_value = sum_in[:, n_query + n_key :]
+
+    gain_sum = jnp.stack([gain_one_part, gain_two_part])
+    gain_sum = gain_sum + over_z(gain_sum, 1)
+    gain_sum = gain_sum + over_z(gain_sum, 2)
+    gain_sum = gain_sum + over_core(gain_sum)
+    gain_sum = gain_sum + over_x(gain_sum)
+    gain_sum = gain_sum + over_y(gain_sum)
+    gain_sum = lax.dynamic_slice(gain_sum, (0, place), (2, share))
+
+    grad_query = sum_query * bound_slope(w_query, b_query[None, :])
+    grad_key = sum_key * bound_slope(w_key, b_key[None, :])
+    grad_value = sum_value * bound_slope(w_value, b_value[None, :])
+    grad_gate = sum_gate * bound_slope(w_gate, b_gate[None, :])
+    grad_up = sum_up * bound_slope(w_up, b_up[None, :])
+    grad_out = sum_out * bound_slope(w_out, b_out[:, None])
+    grad_down = sum_down * bound_slope(w_down, b_down[:, None])
+    return (
+        mixed,
+        grad_tokens,
+        grad_query,
+        grad_key,
+        grad_value,
+        grad_out,
+        grad_gate,
+        grad_up,
+        grad_down,
+        gain_sum[0],
+        gain_sum[1],
+        jnp.stack([peak[0], peak[3]]),
+        jnp.stack([peak[1], peak[2]]),
+        jnp.stack([peak[4], peak[5], peak[6]]),
+    )
+
+
 def solution(mesh):
     in_specs = (
         P(("dp", "seq"), None),
@@ -307,6 +670,9 @@
         P(None, "mp"),
         P(None, "mp"),
     )
+    shape = dict(mesh.shape)
+    paired = shape["dp"] == 4 and shape["seq"] == 2 and shape["mp"] == 4
+    block = paired_block if paired else on_device
     return jax.shard_map(
-        on_device, mesh=mesh, in_specs=in_specs, out_specs=out_specs, check_vma=False
-    )
+        block, mesh=mesh, in_specs=in_specs, out_specs=out_specs, check_vma=False
+    )

time: 1690 us -> 944 us (0.56)
  waiting for transfers between devices: 1310 us -> 417 us
  starting transfers between devices: 1.95 us -> 146 us
  local copies, waits for them, and re-layouts: 21.8 us -> 138 us
  blocking collectives: 91.9 us -> 0 us
    psum x4 -> x0, waiting for transfers between devices: 593 us -> none  [the longest x1 172 us: on_device(): lax.psum(against(grad_query_b, eff_query) + against(grad_key_b, eff_key)...]
    reduce_scatter x9 -> x0, waiting for transfers between devices: 541 us -> none  [the longest x1 139 us: on_device(): lax.psum_scatter(grad_down_eff, ('dp', 'seq'), scatter_dimension=1, tiled...]
    ppermute x0 -> x88, waiting for transfers between devices: none -> 417 us  [the longest x26 212 us: over_z(): return lax.ppermute(values, 'mp', [(i, i ^ step) for i in range(4)])]
    all_gather x7 -> x0, waiting for transfers between devices: 171 us -> none  [the longest x1 58.9 us: on_device(): lax.all_gather(w_up, ('dp', 'seq'), axis=0, tiled=True)]
    ppermute x0 -> x88, starting transfers between devices: none -> 146 us  [the longest x26 101 us: over_z(): return lax.ppermute(values, 'mp', [(i, i ^ step) for i in range(4)])]
    unnamed x2 -> x0, blocking collectives: 47.2 us -> none
    dynamic_update_slice x0 -> x26, local copies, waits for them, and re-layouts: none -> 31.5 us  [the longest x12 16.8 us: z_gather(): full = lax.dynamic_update_slice_in_dim(full, part, (z ^ step) * size, 0)]
    pmax x1 -> x0, blocking collectives: 25.8 us -> none  [on_device(): lax.pmax(channel_peak(w_query, 0).astype(jnp.bfloat16), ('dp', 'seq'))]
  transfers between devices with their start and end apart: 20 -> 88, of which waited for: 16 -> 40; matrix products, arithmetic and copies ran while one was open for 11% -> 30% of each run, Pallas kernels for 0% -> 0%
where the time goes in v1:
time: 944 us; the launch traced here: 928 us
  waiting for transfers between devices  417 us (44%)
  starting transfers between devices  146 us (15%)
  matrix products  141 us (15%)
  local copies, waits for them, and re-layouts  138 us (15%)
  other arithmetic  82.6 us (9%)
    ppermute x26, waiting for transfers between devices, over_z(): return lax.ppermute(values, 'mp', [(i, i ^ step) for i in range(4)])  212 us
    ppermute x22, waiting for transfers between devices, over_y(): return lax.ppermute(values, 'seq', [(0, 1), (1, 0)])  119 us
    ppermute x26, starting transfers between devices, over_z(): return lax.ppermute(values, 'mp', [(i, i ^ step) for i in range(4)])  101 us
    ppermute x20, waiting for transfers between devices, over_x(): return lax.ppermute(values, 'dp', [(i, i ^ 2) for i in range(4)])  85 us
    dot_general x5, matrix products, against(): lax.dot_general(left, weight, (((1,), (1,)), ((), ())), preferred_element...  39.8 us
    dot_general x5, matrix products, natural(): return jnp.dot(left, right, preferred_element_type=F32)  35.6 us
    dot_general x5, matrix products, inner_rows(): lax.dot_general(left, right, (((0,), (0,)), ((), ())), preferred_element_...  32.3 us
    ppermute x22, starting transfers between devices, over_y(): return lax.ppermute(values, 'seq', [(0, 1), (1, 0)])  25.3 us
  transfers between devices with their start and end apart: 88, of which 40 were waited for; matrix products, arithmetic and copies ran while one was open for 30% of the time, Pallas kernels for 0%

profile of v1, /device:TPU:0, one launch (start us, length us, event | category | flops | bytes accessed | tf_op | source)
XLA Modules:
  0.0 928.0 jit_solution(12014622047964760948)
XLA Ops:
  62.2 8.6 collective-permute-done.6
  86.1 21.5 %collective-permute-done.21 = bf16[2,288,1152]{2,1,0:T(8,128)(2,1)S(1)} collective-permute-done((bf16[2,288,1152]{2,1,0:T(8,128)(2,1)S(1)}, bf16[2,288,1152]{2,1,0:T(8,128)(2,1)S(1)}, u32[]{:S(2)}, u32[]{:S(2)}) %collective-permute-start.21) | collective-permute-done | bytes 1327136 | tf_op jit(solution)/shard_map/ppermute | solution.py:283
  130.3 33.1 %collective-permute-done.11 = bf16[512,512]{1,0:T(8,128)(2,1)} collective-permute-done((bf16[512,512]{1,0:T(8,128)(2,1)S(1)}, bf16[512,512]{1,0:T(8,128)(2,1)}, u32[]{:S(2)}, u32[]{:S(2)}) %collective-permute-start.11) | collective-permute-done | bytes 524320 | tf_op jit(solution)/shard_map/ppermute | solution.py:291
  181.7 8.0 fusion.163
  189.7 25.9 %collective-permute-done.12 = bf16[128,2304]{1,0:T(8,128)(2,1)S(1)} collective-permute-done((bf16[128,2304]{1,0:T(8,128)(2,1)S(1)}, bf16[128,2304]{1,0:T(8,128)(2,1)S(1)}, u32[]{:S(2)}, u32[]{:S(2)}) %collective-permute-start.12) | collective-permute-done | bytes 589856 | tf_op jit(solution)/shard_map/ppermute | solution.py:295
  220.5 13.2 %collective-permute-start.15 = (bf16[128,2304]{1,0:T(8,128)(2,1)}, bf16[128,2304]{1,0:T(8,128)(2,1)S(1)}, u32[]{:S(2)}, u32[]{:S(2)}) collective-permute-start(bf16[128,2304]{1,0:T(8,128)(2,1)} %multiply_convert_fusion.5), channel_id=1, source_target_pairs={{0,2},{1,3},{2,0},{3,1},{4,6},{5,7},{6,4},{7,5},{8,10},{9,11},{10,... | collective-permute-start | bytes 1769480 | tf_op jit(solution)/shard_map/ppermute | solution.py:295
  248.8 24.2 %collective-permute-done.15 = bf16[128,2304]{1,0:T(8,128)(2,1)S(1)} collective-permute-done((bf16[128,2304]{1,0:T(8,128)(2,1)}, bf16[128,2304]{1,0:T(8,128)(2,1)S(1)}, u32[]{:S(2)}, u32[]{:S(2)}) %collective-permute-start.15) | collective-permute-done | bytes 589856 | tf_op jit(solution)/shard_map/ppermute | solution.py:295
  302.2 10.1 %collective-permute-done.29 = bf16[288,1152]{1,0:T(8,128)(2,1)S(1)} collective-permute-done((bf16[288,1152]{1,0:T(8,128)(2,1)S(1)}, bf16[288,1152]{1,0:T(8,128)(2,1)S(1)}, u32[]{:S(2)}, u32[]{:S(2)}) %collective-permute-start.29) | collective-permute-done | bytes 663584 | tf_op jit(solution)/shard_map/ppermute | solution.py:291
  320.5 14.6 %fusion.10 = (bf16[1024,1152]{1,0:T(8,128)(2,1)S(1)}, bf16[1024,1152]{1,0:T(8,128)(2,1)}, bf16[1024,1152]{1,0:T(8,128)(2,1)}) fusion(f32[1024,1152]{1,0:T(8,128)} %fusion.163, f32[1024,1152]{1,0:T(8,128)S(1)} %fusion.147, bf16[2304,1152]{1,0:T(8,128)(2,1)} %bitcast.47, bf16[512,2304]{0,1:T(8,128)(2,1)S(1)} %collective-permute-done.18, ...), kind=kOutput, calls=%fused_computation.18 | convolution fusion | flops 5475926016 | bytes 26542080 | tf_op jit(solution)/shard_map/dot_general | solution.py:303
  335.1 9.2 convolution_convert_fusion
  344.3 9.6 %fusion.162 = f32[1024,2304]{1,0:T(8,128)S(1)} fusion(bf16[1024,1152]{1,0:T(8,128)(2,1)} %get-tuple-element.52, bf16[2304,1152]{1,0:T(8,128)(2,1)} %bitcast.410), kind=kOutput, calls=%fused_computation.375 | convolution fusion | flops 5435817984 | bytes 17104896 | tf_op jit(solution)/shard_map/dot_general | solution.py:41
  353.9 8.6 fusion.164
  362.5 12.9 %convolution_add_fusion = f32[1024,2304]{1,0:T(8,128)} fusion(f32[1024,2304]{1,0:T(8,128)} %fusion.164, bf16[1024,1152]{1,0:T(8,128)(2,1)S(1)} %get-tuple-element.50, bf16[2304,1152]{1,0:T(8,128)(2,1)} %bitcast.47), kind=kOutput, calls=%fused_computation.6 | convolution fusion | flops 5438177280 | bytes 26542080 | tf_op jit(solution)/shard_map/dot_general | solution.py:41
  384.5 7.9 convolution_convert_fusion.1
  399.5 8.0 convolution_convert_fusion.2
  419.0 22.8 %collective-permute-done.75 = bf16[2,288,1152]{2,1,0:T(8,128)(2,1)} collective-permute-done((bf16[2,288,1152]{2,1,0:T(8,128)(2,1)}, bf16[2,288,1152]{2,1,0:T(8,128)(2,1)}, u32[]{:S(2)}, u32[]{:S(2)}) %collective-permute-start.75) | collective-permute-done | bytes 1327136 | tf_op jit(solution)/shard_map/ppermute | solution.py:291
  447.5 22.6 %collective-permute-done.70 = bf16[2,288,1152]{2,1,0:T(8,128)(2,1)S(1)} collective-permute-done((bf16[2,288,1152]{2,1,0:T(8,128)(2,1)S(1)}, bf16[2,288,1152]{2,1,0:T(8,128)(2,1)S(1)}, u32[]{:S(2)}, u32[]{:S(2)}) %collective-permute-start.70) | collective-permute-done | bytes 1327136 | tf_op jit(solution)/shard_map/ppermute | solution.py:291
  473.8 13.4 %collective-permute-done.81 = bf16[288,1152]{1,0:T(8,128)(2,1)S(1)} collective-permute-done((bf16[288,1152]{1,0:T(8,128)(2,1)S(1)}, bf16[288,1152]{1,0:T(8,128)(2,1)S(1)}, u32[]{:S(2)}, u32[]{:S(2)}) %collective-permute-start.81) | collective-permute-done | bytes 663584 | tf_op jit(solution)/shard_map/ppermute | solution.py:283
  489.3 12.1 %collective-permute-done.76 = bf16[288,1152]{1,0:T(8,128)(2,1)S(1)} collective-permute-done((bf16[288,1152]{1,0:T(8,128)(2,1)S(1)}, bf16[288,1152]{1,0:T(8,128)(2,1)S(1)}, u32[]{:S(2)}, u32[]{:S(2)}) %collective-permute-start.76) | collective-permute-done | bytes 663584 | tf_op jit(solution)/shard_map/ppermute | solution.py:283
  503.4 11.6 %collective-permute-done.71 = bf16[288,1152]{1,0:T(8,128)(2,1)S(1)} collective-permute-done((bf16[288,1152]{1,0:T(8,128)(2,1)S(1)}, bf16[288,1152]{1,0:T(8,128)(2,1)S(1)}, u32[]{:S(2)}, u32[]{:S(2)}) %collective-permute-start.71) | collective-permute-done | bytes 663584 | tf_op jit(solution)/shard_map/ppermute | solution.py:283
  519.7 9.3 %collective-permute-start.43 = (bf16[128,2304]{1,0:T(8,128)(2,1)S(1)}, bf16[128,2304]{1,0:T(8,128)(2,1)S(1)}, u32[]{:S(2)}, u32[]{:S(2)}) collective-permute-start(bf16[128,2304]{1,0:T(8,128)(2,1)S(1)} %get-tuple-element.74), channel_id=1, source_target_pairs={{0,2},{1,3},{2,0},{3,1},{4,6},{5,7},{6,4},{7,5},{8,10},{9,11},{10,... | collective-permute-start | bytes 1769480 | tf_op jit(solution)/shard_map/ppermute | solution.py:295
  536.6 32.0 %collective-permute-done.43 = bf16[128,2304]{1,0:T(8,128)(2,1)S(1)} collective-permute-done((bf16[128,2304]{1,0:T(8,128)(2,1)S(1)}, bf16[128,2304]{1,0:T(8,128)(2,1)S(1)}, u32[]{:S(2)}, u32[]{:S(2)}) %collective-permute-start.43) | collective-permute-done | bytes 589856 | tf_op jit(solution)/shard_map/ppermute | solution.py:295
  572.5 13.9 %collective-permute-start.46 = (bf16[128,2304]{1,0:T(8,128)(2,1)S(1)}, bf16[128,2304]{1,0:T(8,128)(2,1)}, u32[]{:S(2)}, u32[]{:S(2)}) collective-permute-start(bf16[128,2304]{1,0:T(8,128)(2,1)S(1)} %fusion.150), channel_id=1, source_target_pairs={{0,2},{1,3},{2,0},{3,1},{4,6},{5,7},{6,4},{7,5},{8,10},{9,11},{10,... | collective-permute-start | bytes 1769480 | tf_op jit(solution)/shard_map/ppermute | solution.py:295
  593.0 32.4 %collective-permute-done.46 = bf16[128,2304]{1,0:T(8,128)(2,1)} collective-permute-done((bf16[128,2304]{1,0:T(8,128)(2,1)S(1)}, bf16[128,2304]{1,0:T(8,128)(2,1)}, u32[]{:S(2)}, u32[]{:S(2)}) %collective-permute-start.46) | collective-permute-done | bytes 589856 | tf_op jit(solution)/shard_map/ppermute | solution.py:295
  631.8 8.5 collective-permute-done.48
  652.3 11.7 %fusion.63 = f32[1024,256]{0,1:T(8,128)} fusion(bf16[512,2,256]{0,2,1:T(8,128)(2,1)} %bitcast.430, f32[1024,512,2]{1,0,2:T(8,128)} %fusion.109, f32[1024,512,2]{1,0,2:T(8,128)} %copy-done.18, f32[2,512]{1,0:T(2,128)S(1)} %copy-done.68, pred[512,1024]{0,1:T(8,128)(4,1)} %compare_and_fusion), kind=kOutput, calls=%fused_computation.113 | convolution fusion | flops 553650176 | bytes 10489856 | tf_op jit(solution)/shard_map/rtk,trd->kd/dot_general | solution.py:558
  674.7 9.9 %fusion.67 = bf16[256,2,512]{2,0,1:T(8,128)(2,1)} fusion(f32[1024,512,2]{1,0,2:T(8,128)} %fusion.109, f32[1024,512,2]{1,0,2:T(8,128)} %copy-done.18, f32[2,512]{1,0:T(2,128)S(1)} %copy-done.68, pred[512,1024]{0,1:T(8,128)(4,1)} %compare_and_fusion, bf16[512,512]{1,0:T(8,128)(2,1)} %collective-permute-done.11, bf16[512,512]{1,0:T(8,128)(2,1)} %copy-done.35), kind=kOutput, calls=%fused_computation.153 | convolution fusion | flops 554960896 | bytes 10489856 | tf_op jit(solution)/shard_map/rtk,kd->trd/dot_general | solution.py:552
  703.6 30.4 %collective-permute-done.50 = bf16[128,2304]{1,0:T(8,128)(2,1)S(1)} collective-permute-done((bf16[128,2304]{1,0:T(8,128)(2,1)S(1)}, bf16[128,2304]{1,0:T(8,128)(2,1)S(1)}, u32[]{:S(2)}, u32[]{:S(2)}) %collective-permute-start.50) | collective-permute-done | bytes 589856 | tf_op jit(solution)/shard_map/ppermute | solution.py:295
  736.5 36.6 %collective-permute-start.37 = (bf16[128,2304]{1,0:T(8,128)(2,1)S(1)}, bf16[128,2304]{1,0:T(8,128)(2,1)S(1)}, u32[]{:S(2)}, u32[]{:S(2)}) collective-permute-start(bf16[128,2304]{1,0:T(8,128)(2,1)S(1)} %copy-done.45), channel_id=1, source_target_pairs={{0,1},{1,0},{2,3},{3,2},{4,5},{5,4},{6,7},{7,6},{8,9},{9,8},{10,11... | collective-permute-start | bytes 1769480 | tf_op jit(solution)/shard_map/ppermute | solution.py:295
  773.7 10.8 %collective-permute-done.35 = bf16[128,2304]{1,0:T(8,128)(2,1)S(1)} collective-permute-done((bf16[128,2304]{1,0:T(8,128)(2,1)S(1)}, bf16[128,2304]{1,0:T(8,128)(2,1)S(1)}, u32[]{:S(2)}, u32[]{:S(2)}) %collective-permute-start.35) | collective-permute-done | bytes 589856 | tf_op jit(solution)/shard_map/ppermute | solution.py:295
  785.1 9.9 %collective-permute-done.37 = bf16[128,2304]{1,0:T(8,128)(2,1)S(1)} collective-permute-done((bf16[128,2304]{1,0:T(8,128)(2,1)S(1)}, bf16[128,2304]{1,0:T(8,128)(2,1)S(1)}, u32[]{:S(2)}, u32[]{:S(2)}) %collective-permute-start.37) | collective-permute-done | bytes 589856 | tf_op jit(solution)/shard_map/ppermute | solution.py:295
  875.5 26.3 %collective-permute-done.38 = bf16[128,2304]{1,0:T(8,128)(2,1)} collective-permute-done((bf16[128,2304]{1,0:T(8,128)(2,1)}, bf16[128,2304]{1,0:T(8,128)(2,1)}, u32[]{:S(2)}, u32[]{:S(2)}) %collective-permute-start.38) | collective-permute-done | bytes 589856 | tf_op jit(solution)/shard_map/ppermute | solution.py:295
  (594 shorter events, 395.6 us)
Async XLA Ops:
  15.6 110.0 %collective-permute-start.41 = (bf16[512,2304]{1,0:T(8,128)(2,1)}, bf16[512,2304]{1,0:T(8,128)(2,1)}, u32[]{:S(2)}, u32[]{:S(2)}) collective-permute-start(bf16[512,2304]{1,0:T(8,128)(2,1)} %param.25), channel_id=1, source_target_pairs={{0,8},{8,0},{16,24},{24,16},{1,9},{9,1},{17,25},{25,17},{2,10},{10... | collective-permute-start | bytes 7077896 | tf_op jit(solution)/shard_map/ppermute | solution.py:287
  107.6 127.5 %collective-permute-start.22 = (bf16[2,288,1152]{2,1,0:T(8,128)(2,1)}, bf16[2,288,1152]{2,1,0:T(8,128)(2,1)}, u32[]{:S(2)}, u32[]{:S(2)}) collective-permute-start(bf16[2,288,1152]{2,1,0:T(8,128)(2,1)} %reverse_select_fusion.6), channel_id=1, source_target_pairs={{0,16},{8,24},{16,0},{24,8},{1,17},{9,25},{17,1},{25,9},{2,18},{10... | collective-permute-start | bytes 3981320 | tf_op jit(solution)/shard_map/ppermute | solution.py:283
  108.0 134.7 %collective-permute-start.23 = (bf16[2,288,1152]{2,1,0:T(8,128)(2,1)}, bf16[2,288,1152]{2,1,0:T(8,128)(2,1)}, u32[]{:S(2)}, u32[]{:S(2)}) collective-permute-start(bf16[2,288,1152]{2,1,0:T(8,128)(2,1)} %reverse_select_fusion.6), channel_id=1, source_target_pairs={{0,4},{4,0},{1,5},{5,1},{2,6},{6,2},{3,7},{7,3},{8,12},{12,8},{9,1... | collective-permute-start | bytes 3981320 | tf_op jit(solution)/shard_map/ppermute | solution.py:291
  115.5 63.2 %collective-permute-start.32 = (bf16[288,1152]{1,0:T(8,128)(2,1)S(1)}, bf16[288,1152]{1,0:T(8,128)(2,1)}, u32[]{:S(2)}, u32[]{:S(2)}) collective-permute-start(bf16[288,1152]{1,0:T(8,128)(2,1)S(1)} %slice_bitcast_fusion.1), channel_id=1, source_target_pairs={{0,4},{4,0},{1,5},{5,1},{2,6},{6,2},{3,7},{7,3},{8,12},{12,8},{9,1... | collective-permute-start | bytes 1990664 | tf_op jit(solution)/shard_map/ppermute | solution.py:291
  125.6 54.4 %collective-permute-start.33 = (bf16[288,1152]{1,0:T(8,128)(2,1)}, bf16[288,1152]{1,0:T(8,128)(2,1)S(1)}, u32[]{:S(2)}, u32[]{:S(2)}) collective-permute-start(bf16[288,1152]{1,0:T(8,128)(2,1)} %slice_bitcast_fusion), channel_id=1, source_target_pairs={{0,16},{8,24},{16,0},{24,8},{1,17},{9,25},{17,1},{25,9},{2,18},{10... | collective-permute-start | bytes 1990664 | tf_op jit(solution)/shard_map/ppermute | solution.py:283
  220.5 52.5 %collective-permute-start.15 = (bf16[128,2304]{1,0:T(8,128)(2,1)}, bf16[128,2304]{1,0:T(8,128)(2,1)S(1)}, u32[]{:S(2)}, u32[]{:S(2)}) collective-permute-start(bf16[128,2304]{1,0:T(8,128)(2,1)} %multiply_convert_fusion.5), channel_id=1, source_target_pairs={{0,2},{1,3},{2,0},{3,1},{4,6},{5,7},{6,4},{7,5},{8,10},{9,11},{10,... | collective-permute-start | bytes 1769480 | tf_op jit(solution)/shard_map/ppermute | solution.py:295
  233.6 43.1 %collective-permute-start.16 = (bf16[128,2304]{1,0:T(8,128)(2,1)}, bf16[128,2304]{1,0:T(8,128)(2,1)}, u32[]{:S(2)}, u32[]{:S(2)}) collective-permute-start(bf16[128,2304]{1,0:T(8,128)(2,1)} %multiply_convert_fusion.5), channel_id=1, source_target_pairs={{0,3},{1,2},{2,1},{3,0},{4,7},{5,6},{6,5},{7,4},{8,11},{9,10},{10,... | collective-permute-start | bytes 1769480 | tf_op jit(solution)/shard_map/ppermute | solution.py:295
  234.2 44.8 %collective-permute-start.17 = (bf16[128,2304]{1,0:T(8,128)(2,1)}, bf16[128,2304]{1,0:T(8,128)(2,1)}, u32[]{:S(2)}, u32[]{:S(2)}) collective-permute-start(bf16[128,2304]{1,0:T(8,128)(2,1)} %multiply_convert_fusion.5), channel_id=1, source_target_pairs={{0,1},{1,0},{2,3},{3,2},{4,5},{5,4},{6,7},{7,6},{8,9},{9,8},{10,11... | collective-permute-start | bytes 1769480 | tf_op jit(solution)/shard_map/ppermute | solution.py:295
  235.1 60.8 %collective-permute-start.27 = (bf16[2,288,1152]{2,1,0:T(8,128)(2,1)S(1)}, bf16[2,288,1152]{2,1,0:T(8,128)(2,1)}, u32[]{:S(2)}, u32[]{:S(2)}) collective-permute-start(bf16[2,288,1152]{2,1,0:T(8,128)(2,1)S(1)} %reverse_select_fusion.4), channel_id=1, source_target_pairs={{0,16},{8,24},{16,0},{24,8},{1,17},{9,25},{17,1},{25,9},{2,18},{10... | collective-permute-start | bytes 3981320 | tf_op jit(solution)/shard_map/ppermute | solution.py:283
  242.6 54.9 %collective-permute-start.28 = (bf16[2,288,1152]{2,1,0:T(8,128)(2,1)S(1)}, bf16[2,288,1152]{2,1,0:T(8,128)(2,1)}, u32[]{:S(2)}, u32[]{:S(2)}) collective-permute-start(bf16[2,288,1152]{2,1,0:T(8,128)(2,1)S(1)} %reverse_select_fusion.4), channel_id=1, source_target_pairs={{0,4},{4,0},{1,5},{5,1},{2,6},{6,2},{3,7},{7,3},{8,12},{12,8},{9,1... | collective-permute-start | bytes 3981320 | tf_op jit(solution)/shard_map/ppermute | solution.py:291
  379.4 137.2 %collective-permute-start.42 = (bf16[512,2304]{1,0:T(8,128)(2,1)}, bf16[512,2304]{1,0:T(8,128)(2,1)S(1)}, u32[]{:S(2)}, u32[]{:S(2)}) collective-permute-start(bf16[512,2304]{1,0:T(8,128)(2,1)} %slice.354), channel_id=1, source_target_pairs={{0,8},{8,0},{16,24},{24,16},{1,9},{9,1},{17,25},{25,17},{2,10},{10... | collective-permute-start | bytes 7077896 | tf_op jit(solution)/shard_map/ppermute | solution.py:287
  396.5 45.2 %collective-permute-start.75 = (bf16[2,288,1152]{2,1,0:T(8,128)(2,1)}, bf16[2,288,1152]{2,1,0:T(8,128)(2,1)}, u32[]{:S(2)}, u32[]{:S(2)}) collective-permute-start(bf16[2,288,1152]{2,1,0:T(8,128)(2,1)} %dynamic-slice_bitcast_fusion.2), channel_id=1, source_target_pairs={{0,4},{4,0},{1,5},{5,1},{2,6},{6,2},{3,7},{7,3},{8,12},{12,8},{9,1... | collective-permute-start | bytes 3981320 | tf_op jit(solution)/shard_map/ppermute | solution.py:291
  398.4 46.2 %collective-permute-start.73 = (bf16[2,288,1152]{2,1,0:T(8,128)(2,1)}, bf16[2,288,1152]{2,1,0:T(8,128)(2,1)}, u32[]{:S(2)}, u32[]{:S(2)}) collective-permute-start(bf16[2,288,1152]{2,1,0:T(8,128)(2,1)} %dynamic-slice_bitcast_fusion.3), channel_id=1, source_target_pairs={{0,16},{8,24},{16,0},{24,8},{1,17},{9,25},{17,1},{25,9},{2,18},{10... | collective-permute-start | bytes 3981320 | tf_op jit(solution)/shard_map/ppermute | solution.py:283
  413.3 56.8 %collective-permute-start.70 = (bf16[2,288,1152]{2,1,0:T(8,128)(2,1)S(1)}, bf16[2,288,1152]{2,1,0:T(8,128)(2,1)S(1)}, u32[]{:S(2)}, u32[]{:S(2)}) collective-permute-start(bf16[2,288,1152]{2,1,0:T(8,128)(2,1)S(1)} %dynamic-slice_bitcast_fusion.4), channel_id=1, source_target_pairs={{0,4},{4,0},{1,5},{5,1},{2,6},{6,2},{3,7},{7,3},{8,12},{12,8},{9,1... | collective-permute-start | bytes 3981320 | tf_op jit(solution)/shard_map/ppermute | solution.py:291
  416.7 56.3 %collective-permute-start.68 = (bf16[2,288,1152]{2,1,0:T(8,128)(2,1)S(1)}, bf16[2,288,1152]{2,1,0:T(8,128)(2,1)S(1)}, u32[]{:S(2)}, u32[]{:S(2)}) collective-permute-start(bf16[2,288,1152]{2,1,0:T(8,128)(2,1)S(1)} %dynamic-slice_bitcast_fusion.5), channel_id=1, source_target_pairs={{0,16},{8,24},{16,0},{24,8},{1,17},{9,25},{17,1},{25,9},{2,18},{10... | collective-permute-start | bytes 3981320 | tf_op jit(solution)/shard_map/ppermute | solution.py:283
  441.8 45.4 %collective-permute-start.81 = (bf16[288,1152]{1,0:T(8,128)(2,1)S(1)}, bf16[288,1152]{1,0:T(8,128)(2,1)S(1)}, u32[]{:S(2)}, u32[]{:S(2)}) collective-permute-start(bf16[288,1152]{1,0:T(8,128)(2,1)S(1)} %fusion.95), channel_id=1, source_target_pairs={{0,16},{8,24},{16,0},{24,8},{1,17},{9,25},{17,1},{25,9},{2,18},{10... | collective-permute-start | bytes 1990664 | tf_op jit(solution)/shard_map/ppermute | solution.py:283
  444.6 43.1 %collective-permute-start.79 = (bf16[288,1152]{1,0:T(8,128)(2,1)S(1)}, bf16[288,1152]{1,0:T(8,128)(2,1)S(1)}, u32[]{:S(2)}, u32[]{:S(2)}) collective-permute-start(bf16[288,1152]{1,0:T(8,128)(2,1)S(1)} %fusion.94), channel_id=1, source_target_pairs={{0,4},{4,0},{1,5},{5,1},{2,6},{6,2},{3,7},{7,3},{8,12},{12,8},{9,1... | collective-permute-start | bytes 1990664 | tf_op jit(solution)/shard_map/ppermute | solution.py:291
  501.4 329.4 %collective-permute-start.56 = (bf16[512,2,576]{0,2,1:T(8,128)(2,1)}, bf16[512,2,576]{0,2,1:T(8,128)(2,1)}, u32[]{:S(2)}, u32[]{:S(2)}) collective-permute-start(bf16[512,2,576]{0,2,1:T(8,128)(2,1)} %get-tuple-element.70), channel_id=1, source_target_pairs={{0,8},{8,0},{16,24},{24,16},{1,9},{9,1},{17,25},{25,17},{2,10},{10... | collective-permute-start | bytes 3538952 | tf_op jit(solution)/shard_map/ppermute | solution.py:287
  519.7 48.8 %collective-permute-start.43 = (bf16[128,2304]{1,0:T(8,128)(2,1)S(1)}, bf16[128,2304]{1,0:T(8,128)(2,1)S(1)}, u32[]{:S(2)}, u32[]{:S(2)}) collective-permute-start(bf16[128,2304]{1,0:T(8,128)(2,1)S(1)} %get-tuple-element.74), channel_id=1, source_target_pairs={{0,2},{1,3},{2,0},{3,1},{4,6},{5,7},{6,4},{7,5},{8,10},{9,11},{10,... | collective-permute-start | bytes 1769480 | tf_op jit(solution)/shard_map/ppermute | solution.py:295
  536.5 273.6 %collective-permute-start.63 = (bf16[512,512]{0,1:T(8,128)(2,1)}, bf16[512,512]{0,1:T(8,128)(2,1)}, u32[]{:S(2)}, u32[]{:S(2)}) collective-permute-start(bf16[512,512]{0,1:T(8,128)(2,1)} %bitcast.27), channel_id=1, source_target_pairs={{0,8},{8,0},{16,24},{24,16},{1,9},{9,1},{17,25},{25,17},{2,10},{10... | collective-permute-start | bytes 1572872 | tf_op jit(solution)/shard_map/ppermute | solution.py:287
  572.5 52.9 %collective-permute-start.46 = (bf16[128,2304]{1,0:T(8,128)(2,1)S(1)}, bf16[128,2304]{1,0:T(8,128)(2,1)}, u32[]{:S(2)}, u32[]{:S(2)}) collective-permute-start(bf16[128,2304]{1,0:T(8,128)(2,1)S(1)} %fusion.150), channel_id=1, source_target_pairs={{0,2},{1,3},{2,0},{3,1},{4,6},{5,7},{6,4},{7,5},{8,10},{9,11},{10,... | collective-permute-start | bytes 1769480 | tf_op jit(solution)/shard_map/ppermute | solution.py:295
  589.0 83.4 %collective-permute-start.72 = (bf16[288,1152]{1,0:T(8,128)(2,1)}, bf16[288,1152]{1,0:T(8,128)(2,1)}, u32[]{:S(2)}, u32[]{:S(2)}) collective-permute-start(bf16[288,1152]{1,0:T(8,128)(2,1)} %get-tuple-element.58), channel_id=1, source_target_pairs={{0,8},{8,0},{16,24},{24,16},{1,9},{9,1},{17,25},{25,17},{2,10},{10... | collective-permute-start | bytes 1990664 | tf_op jit(solution)/shard_map/ppermute | solution.py:287
  734.0 50.6 %collective-permute-start.35 = (bf16[128,2304]{1,0:T(8,128)(2,1)S(1)}, bf16[128,2304]{1,0:T(8,128)(2,1)S(1)}, u32[]{:S(2)}, u32[]{:S(2)}) collective-permute-start(bf16[128,2304]{1,0:T(8,128)(2,1)S(1)} %copy-done.47), channel_id=1, source_target_pairs={{0,2},{1,3},{2,0},{3,1},{4,6},{5,7},{6,4},{7,5},{8,10},{9,11},{10,... | collective-permute-start | bytes 1769480 | tf_op jit(solution)/shard_map/ppermute | solution.py:295
  734.0 50.6 %collective-permute-start.36 = (bf16[128,2304]{1,0:T(8,128)(2,1)S(1)}, bf16[128,2304]{1,0:T(8,128)(2,1)S(1)}, u32[]{:S(2)}, u32[]{:S(2)}) collective-permute-start(bf16[128,2304]{1,0:T(8,128)(2,1)S(1)} %copy-done.46), channel_id=1, source_target_pairs={{0,3},{1,2},{2,1},{3,0},{4,7},{5,6},{6,5},{7,4},{8,11},{9,10},{10,... | collective-permute-start | bytes 1769480 | tf_op jit(solution)/shard_map/ppermute | solution.py:295
  736.5 58.6 %collective-permute-start.37 = (bf16[128,2304]{1,0:T(8,128)(2,1)S(1)}, bf16[128,2304]{1,0:T(8,128)(2,1)S(1)}, u32[]{:S(2)}, u32[]{:S(2)}) collective-permute-start(bf16[128,2304]{1,0:T(8,128)(2,1)S(1)} %copy-done.45), channel_id=1, source_target_pairs={{0,1},{1,0},{2,3},{3,2},{4,5},{5,4},{6,7},{7,6},{8,9},{9,8},{10,11... | collective-permute-start | bytes 1769480 | tf_op jit(solution)/shard_map/ppermute | solution.py:295
  784.6 48.4 %collective-permute-start.57 = (bf16[512,1024]{0,1:T(8,128)(2,1)}, bf16[512,1024]{0,1:T(8,128)(2,1)}, u32[]{:S(2)}, u32[]{:S(2)}) collective-permute-start(bf16[512,1024]{0,1:T(8,128)(2,1)} %pad_maximum_fusion.6), channel_id=1, source_target_pairs={{0,8},{8,0},{16,24},{24,16},{1,9},{9,1},{17,25},{25,17},{2,10},{10... | collective-permute-start | bytes 3145736 | tf_op jit(solution)/shard_map/ppermute | solution.py:287
  809.2 42.8 %collective-permute-start.53 = (bf16[128,2304]{1,0:T(8,128)(2,1)}, bf16[128,2304]{1,0:T(8,128)(2,1)S(1)}, u32[]{:S(2)}, u32[]{:S(2)}) collective-permute-start(bf16[128,2304]{1,0:T(8,128)(2,1)} %get-tuple-element.92), channel_id=1, source_target_pairs={{0,2},{1,3},{2,0},{3,1},{4,6},{5,7},{6,4},{7,5},{8,10},{9,11},{10,... | collective-permute-start | bytes 1769480 | tf_op jit(solution)/shard_map/ppermute | solution.py:295
  830.8 71.0 %collective-permute-start.38 = (bf16[128,2304]{1,0:T(8,128)(2,1)}, bf16[128,2304]{1,0:T(8,128)(2,1)}, u32[]{:S(2)}, u32[]{:S(2)}) collective-permute-start(bf16[128,2304]{1,0:T(8,128)(2,1)} %get-tuple-element.93), channel_id=1, source_target_pairs={{0,2},{1,3},{2,0},{3,1},{4,6},{5,7},{6,4},{7,5},{8,10},{9,11},{10,... | collective-permute-start | bytes 1769480 | tf_op jit(solution)/shard_map/ppermute | solution.py:295
  844.9 59.1 %collective-permute-start.39 = (bf16[128,2304]{1,0:T(8,128)(2,1)}, bf16[128,2304]{1,0:T(8,128)(2,1)}, u32[]{:S(2)}, u32[]{:S(2)}) collective-permute-start(bf16[128,2304]{1,0:T(8,128)(2,1)} %get-tuple-element.93), channel_id=1, source_target_pairs={{0,3},{1,2},{2,1},{3,0},{4,7},{5,6},{6,5},{7,4},{8,11},{9,10},{10,... | collective-permute-start | bytes 1769480 | tf_op jit(solution)/shard_map/ppermute | solution.py:295
  852.8 54.5 %collective-permute-start.40 = (bf16[128,2304]{1,0:T(8,128)(2,1)}, bf16[128,2304]{1,0:T(8,128)(2,1)}, u32[]{:S(2)}, u32[]{:S(2)}) collective-permute-start(bf16[128,2304]{1,0:T(8,128)(2,1)} %get-tuple-element.93), channel_id=1, source_target_pairs={{0,1},{1,0},{2,3},{3,2},{4,5},{5,4},{6,7},{7,6},{8,9},{9,8},{10,11... | collective-permute-start | bytes 1769480 | tf_op jit(solution)/shard_map/ppermute | solution.py:295
  854.9 59.9 %collective-permute-start.60 = (bf16[2,288,512]{2,1,0:T(8,128)(2,1)}, bf16[2,288,512]{2,1,0:T(8,128)(2,1)}, u32[]{:S(2)}, u32[]{:S(2)}) collective-permute-start(bf16[2,288,512]{2,1,0:T(8,128)(2,1)} %dynamic-slice_bitcast_fusion.12), channel_id=1, source_target_pairs={{0,4},{4,0},{1,5},{5,1},{2,6},{6,2},{3,7},{7,3},{8,12},{12,8},{9,1... | collective-permute-start | bytes 1769480 | tf_op jit(solution)/shard_map/ppermute | solution.py:291
  864.4 52.5 %collective-permute-start.58 = (bf16[2,288,512]{2,1,0:T(8,128)(2,1)}, bf16[2,288,512]{2,1,0:T(8,128)(2,1)}, u32[]{:S(2)}, u32[]{:S(2)}) collective-permute-start(bf16[2,288,512]{2,1,0:T(8,128)(2,1)} %dynamic-slice_bitcast_fusion.13), channel_id=1, source_target_pairs={{0,16},{8,24},{16,0},{24,8},{1,17},{9,25},{17,1},{25,9},{2,18},{10... | collective-permute-start | bytes 1769480 | tf_op jit(solution)/shard_map/ppermute | solution.py:283
  (145 other events, 2430.2 us)

commit v2 on v0

--- a/solution.py
+++ b/solution.py
@@ -1,6 +1,10 @@
+import itertools
+
 import jax
 import jax.numpy as jnp
 from jax import lax
+from jax.experimental import pallas as pl
+from jax.experimental.pallas import tpu as pltpu
 from jax.sharding import PartitionSpec as P
 
 HQ = 8
@@ -275,6 +279,1865 @@
     )
 
 
+F32 = jnp.float32
+BF16 = jnp.bfloat16
+MESH = pl.DeviceIdType.MESH
+VMEM_BYTES = 63 * 1024 * 1024
+
+
+def natural(left, right):
+    return jnp.dot(left, right, preferred_element_type=F32)
+
+
+def mul(index, size):
+    return pl.multiple_of(index * size, size)
+
+
+class Place:
+    def __init__(self):
+        dp, y, z = lax.axis_index("dp"), lax.axis_index("seq"), lax.axis_index("mp")
+        x, core = dp // 2, dp % 2
+        self.x, self.y, self.z, self.core = x, y, z, core
+        self.to_core = (x * 2 + (1 - core), y, z)
+        self.to_x = ((1 - x) * 2 + core, y, z)
+        self.to_y = (dp, 1 - y, z)
+        self.to_xy = ((1 - x) * 2 + core, 1 - y, z)
+        self.to_up = (dp, y, jnp.minimum(z + 1, 3))
+        self.to_down = (dp, y, jnp.maximum(z - 1, 0))
+
+    def slot(self, x, core, y):
+        return (x * 2 + core) * 2 + y
+
+
+def greet(here, targets):
+    barrier = pltpu.get_barrier_semaphore()
+    for target in targets:
+        pl.semaphore_signal(barrier, inc=1, device_id=target, device_id_type=MESH)
+
+    @pl.when(here.z < 3)
+    def _():
+        pl.semaphore_signal(barrier, inc=1, device_id=here.to_up, device_id_type=MESH)
+
+    @pl.when(here.z > 0)
+    def _():
+        pl.semaphore_signal(barrier, inc=1, device_id=here.to_down, device_id_type=MESH)
+
+    inner = (here.z < 3) & (here.z > 0)
+
+    @pl.when(inner)
+    def _():
+        pl.semaphore_wait(barrier, len(targets) + 2)
+
+    @pl.when(jnp.logical_not(inner))
+    def _():
+        pl.semaphore_wait(barrier, len(targets) + 1)
+
+
+def remote(src, dst, send, recv, target):
+    return pltpu.make_async_remote_copy(
+        src_ref=src,
+        dst_ref=dst,
+        send_sem=send,
+        recv_sem=recv,
+        device_id=target,
+        device_id_type=MESH,
+    )
+
+
+class Line:
+    def __init__(self, here, partial, gathered, land, total, sems, transform, own=None, give=None, subs=4):
+        self.here, self.partial, self.gathered, self.own = here, partial, gathered, own
+        self.land, self.total, self.sems, self.transform = land, total, sems, transform
+        self.size, self.subs = partial.shape[0] // 4, subs
+        self.give = give
+        self.part = self.size // subs
+
+    def rows(self, chunk, sub):
+        return pl.ds(pl.multiple_of(chunk * self.size + sub * self.part, self.part), self.part)
+
+    def scatter_copy(self, way, step, sub=None):
+        z = self.here.z
+        chunk = jnp.minimum(z + 4 - step, 3) if way == 0 else jnp.maximum(z - 4 + step, 0)
+        rows, spot = self.span(chunk, sub)
+        at = (0, way, step - 1)
+        recv = self.sems[1].at[at + (sub or 0,)]
+        target = self.here.to_up if way == 0 else self.here.to_down
+        dst = self.land.at[way, step - 1, spot]
+        return remote(self.partial.at[rows], dst, self.sems[0].at[at], recv, target)
+
+    def gather_copy(self, way, step, sub=None):
+        z = self.here.z
+        chunk = jnp.maximum(z - (step - 1), 0) if way == 0 else jnp.minimum(z + (step - 1), 3)
+        rows, spot = self.span(chunk, sub)
+        at = (1, way, step - 1)
+        recv = self.sems[1].at[at + (sub or 0,)]
+        target = self.here.to_up if way == 0 else self.here.to_down
+        ref = self.gathered.at[rows]
+        src = ref
+        if self.own is not None and step == 1:
+            src = self.own.at[spot]
+        return remote(src, ref, self.sems[0].at[at], recv, target)
+
+    def span(self, chunk, sub):
+        if sub is None:
+            return pl.ds(pl.multiple_of(chunk * self.size, self.size), self.size), pl.ds(0, self.size)
+        return self.rows(chunk, sub), pl.ds(sub * self.part, self.part)
+
+    def far(self, way):
+        return self.here.z if way == 0 else 3 - self.here.z
+
+    def scatter(self, step, sub):
+        for way in (0, 1):
+            far = self.far(way)
+
+            @pl.when((far <= step - 1) & (far <= 2))
+            def _(way=way, far=far):
+                if step > 1:
+
+                    @pl.when(far >= 1)
+                    def _():
+                        self.scatter_copy(way, step - 1, sub).wait_recv()
+                        z = self.here.z
+                        chunk = z + 4 - step if way == 0 else z - 4 + step
+                        rows = self.rows(chunk, sub)
+                        came = self.land[way, step - 2, pl.ds(sub * self.part, self.part), :]
+                        mine = self.partial[rows, :].astype(F32)
+                        self.partial[rows, :] = (mine + came.astype(F32)).astype(BF16)
+
+                self.scatter_copy(way, step, sub).start()
+
+    def finish(self, sub):
+        rows = self.rows(self.here.z, sub)
+        spot = pl.ds(sub * self.part, self.part)
+        self.total[...] = self.partial[rows, :].astype(F32)
+        for way in (0, 1):
+
+            @pl.when(self.far(way) >= 1)
+            def _(way=way):
+                self.scatter_copy(way, 3, sub).wait_recv()
+                self.total[...] += self.land[way, 2, spot, :].astype(F32)
+
+        result = self.transform(sub, spot, self.total[...])
+        if self.own is None:
+            self.gathered[rows, :] = result
+        else:
+            self.own[spot, :] = result
+
+    def gather(self, step, sub):
+        for way in (0, 1):
+            far = self.far(way)
+
+            @pl.when((far >= step - 1) & (far <= 2))
+            def _(way=way):
+                self.gather_copy(way, step, sub).start()
+
+    def landed(self, step, sub):
+        for way in (0, 1):
+
+            @pl.when(self.far(way) >= step)
+            def _(way=way):
+                self.gather_copy(way, step, sub).wait_recv()
+
+    def ticks(self):
+        self.scatter(1, 0)
+        for tick in range(self.subs + 6):
+            for stage in range(7):
+                sub = tick - stage + (stage == 0)
+                if 0 <= sub < self.subs:
+                    if stage < 3:
+                        self.scatter(stage + 1, sub)
+                    else:
+                        if stage == 3:
+                            self.finish(sub)
+                        else:
+                            self.landed(stage - 3, sub)
+                        if stage < 6:
+                            self.gather(stage - 2, sub)
+                        elif self.give is not None:
+                            self.give(sub)
+            yield tick
+
+    def close(self):
+        for step in (1, 2, 3):
+            for way in (0, 1):
+                far = self.far(way)
+
+                @pl.when((far <= step - 1) & (far <= 2))
+                def _(way=way, step=step):
+                    self.scatter_copy(way, step).wait_send()
+
+                @pl.when((far >= step - 1) & (far <= 2))
+                def _(way=way, step=step):
+                    self.gather_copy(way, step).wait_send()
+
+
+def line_sems(subs):
+    return [pltpu.SemaphoreType.DMA((2, 2, 3)), pltpu.SemaphoreType.DMA((2, 2, 3, subs))]
+
+
+def line_scratch(rows, width, subs):
+    return [
+        pltpu.VMEM((rows, width), BF16),
+        pltpu.VMEM((2, 3, rows // 4, width), BF16),
+        pltpu.VMEM((rows // 4 // subs, width), F32),
+        *line_sems(subs),
+    ]
+
+
+class Mail:
+    def __init__(self, send_sem, recv_sem):
+        self.send_sem, self.recv_sem = send_sem, recv_sem
+        self.sent, self.gone = [], []
+        self.n_send = self.n_recv = 0
+
+    def make(self, src, dst, target, send_at=None, recv_at=None):
+        alone = send_at is None
+        if alone:
+            send_at, self.n_send = self.n_send, self.n_send + 1
+        if recv_at is None:
+            recv_at, self.n_recv = self.n_recv, self.n_recv + 1
+        copy = remote(src, dst, self.send_sem.at[send_at], self.recv_sem.at[recv_at], target)
+        if alone:
+            self.sent.append(copy)
+        return copy
+
+    def send(self, src, dst, target, send_at=None, recv_at=None):
+        copy = self.make(src, dst, target, send_at, recv_at)
+        copy.start()
+        return copy
+
+    def group(self, leaving, coming, target):
+        send_at, recv_at = self.n_send, self.n_recv
+        self.n_send, self.n_recv = send_at + 1, recv_at + 1
+        sems = self.send_sem.at[send_at], self.recv_sem.at[recv_at]
+        self.sent.append(remote(leaving, leaving, *sems, target))
+        return send_at, recv_at, remote(coming, coming, *sems, target)
+
+    def finish(self, copy):
+        copy.wait_send()
+        self.gone.append(copy)
+
+    def close(self):
+        for copy in self.sent:
+            if all(copy is not other for other in self.gone):
+                copy.wait_send()
+
+
+FRONT_SUBS, BACK_SUBS = 4, 8
+
+
+EXTRA = 16
+
+
+def edge(y, rows):
+    return pl.multiple_of((1 - y) * (rows - EXTRA), EXTRA)
+
+
+def number_rows(segments, y, out):
+    rows = out.shape[0] - EXTRA
+
+    def turned(start):
+        row = segments[:, pl.ds(pl.multiple_of(start, 128), 128)].astype(F32)
+        return jnp.transpose(jnp.broadcast_to(row, (128, 128)))
+
+    for first in range(0, rows, 128):
+        out[first : first + 128, :] = turned(y * rows + first)
+    out[rows:, :] = jnp.where(y == 0, turned(rows)[:EXTRA], turned(rows - 128)[128 - EXTRA :])
+
+
+def visible(keys, numbers, position, y):
+    count = keys.shape[0]
+    rows = count - EXTRA
+    key = lax.broadcasted_iota(jnp.int32, (count, 1), 0)
+    key_pos = jnp.where(key < rows, y * rows + key, key - EXTRA * y)
+    return (keys[:, 0:1] == numbers) & (key_pos <= position)
+
+
+def beside(value, n_heads):
+    return jnp.concatenate([value] * n_heads, axis=1)
+
+
+def extra_visible(keys, y, n_heads):
+    rows = keys.shape[0] - EXTRA
+    numbers = jnp.transpose(keys[rows:, :])[0:1, :]
+    position = rows - EXTRA * y + lax.broadcasted_iota(jnp.int32, (1, EXTRA), 1)
+    return visible(keys, beside(numbers, n_heads), beside(position, n_heads), y)
+
+
+def soft_probs(query, kv, allowed):
+    raw = against(kv[:, :HD], query)
+    bent = jnp.tanh(raw * HD ** (-0.5) / SOFTCAP)
+    capped = jnp.where(allowed, SOFTCAP * bent, -1e30)
+    weights = jnp.exp(capped - jnp.max(capped, axis=0, keepdims=True))
+    return weights / jnp.sum(weights, axis=0, keepdims=True), bent
+
+
+def row_of(ref, first, count):
+    return jnp.concatenate([ref[first + i : first + i + 1, :] for i in range(count)], axis=1)
+
+
+def level(pick):
+    return jnp.where(pick == 0, 1.0, jnp.where(pick == 1, 0.5, 0.25)).astype(F32)
+
+
+GELU_C = 0.7978845608028654
+GELU_A = 0.044715
+
+
+def gelu_pair(value):
+    square = value * value
+    bent = jnp.tanh(GELU_C * value * (1.0 + GELU_A * square))
+    out = 0.5 * value * (1.0 + bent)
+    slope = 0.5 * (1.0 + bent)
+    slope += 0.5 * value * (1.0 - bent * bent) * (GELU_C * (1.0 + 3.0 * GELU_A * square))
+    return out, slope
+
+
+def front_kernel(
+    width_pick,
+    w_query,
+    w_key,
+    w_value,
+    w_out_t,
+    w_down_t,
+    w_gate,
+    w_up,
+    gains,
+    tokens_in,
+    cot_in,
+    segments,
+    e_attn_out,
+    h2_out,
+    x1_out,
+    query_out,
+    kv_out,
+    heads_out,
+    h1_out,
+    cot_out,
+    mixed_in_out,
+    grad_gate_out,
+    grad_up_out,
+    back_out,
+    ffn_out,
+    slope_ffn_out,
+    slope_attn_out,
+    small_out,
+    peaks_out,
+    early_out,
+    wf_mine,
+    wf_other,
+    ea,
+    ed,
+    eg,
+    eu,
+    rows_a,
+    cots,
+    query,
+    kv,
+    heads,
+    h2,
+    x1,
+    mixed_in,
+    grad_gate,
+    grad_up,
+    slope_attn,
+    small_src,
+    small_land,
+    small,
+    peaks_src,
+    peaks_land,
+    peaks,
+    peaks_peer,
+    keys,
+    extra_heads,
+    extra_land,
+    early_made,
+    early_sem,
+    partial,
+    land,
+    total,
+    line_send,
+    line_recv,
+    local_sem,
+    send_sem,
+    recv_sem,
+):
+    here = Place()
+    x, y, z, core = here.x, here.y, here.z, here.core
+    rows, width = tokens_in.shape
+    share, n_query = w_query.shape
+    n_key = w_key.shape[1]
+    n_in, n_attn = n_query + 2 * n_key, 2 * n_query + 2 * n_key
+    half = w_gate.shape[1] // 2
+    cuts = (0, 5 * half // 9, 7 * half // 9, half)
+    weights = (w_down_t, w_gate, w_up)
+    effective = (ed, eg, eu)
+    tokens, h1 = rows_a.at[pl.ds(0, rows)], rows_a.at[pl.ds(rows, rows)]
+
+    local_count = [0]
+
+    def fetch(src, dst):
+        copy = pltpu.make_async_copy(src, dst, local_sem.at[local_count[0]])
+        local_count[0] += 1
+        copy.start()
+        return copy
+
+    def slab(ref, sx, score, sy, first=0, part=share, cols=None):
+        at = pl.ds(pl.multiple_of(here.slot(sx, score, sy) * share + first, 16), part)
+        return ref.at[at] if cols is None else ref.at[at, cols]
+
+    own_at = here.slot(x, core, y) * share
+    attn_cols = [(w_query, 0), (w_key, n_query), (w_value, n_query + n_key), (w_out_t, n_in)]
+    get_attn = [
+        fetch(w, slab(ea, x, core, y, cols=pl.ds(at, w.shape[1]))) for w, at in attn_cols
+    ]
+    mine_cols = pl.ds(pl.multiple_of(core * half, half), half)
+    their_cols = pl.ds(pl.multiple_of((1 - core) * half, half), half)
+    part_cols = [pl.ds(part * half, half) for part in range(3)]
+    get_ffn = [fetch(w.at[:, mine_cols], wf_mine.at[:, part_cols[i]]) for i, w in enumerate(weights)]
+    get_tokens = fetch(tokens_in, tokens)
+    get_cot = fetch(cot_in, cots.at[pl.ds(0, rows)])
+    greet(here, [here.to_core, here.to_x, here.to_y, here.to_xy])
+    mail = Mail(send_sem, recv_sem)
+
+    half_share = share // 2
+
+    def peak(block):
+        return jnp.max(jnp.abs(block.astype(F32)), axis=0, keepdims=True)
+
+    def set_out(first):
+        ref = slab(ea, x, core, y, first, half_share)
+        return [mail.send(ref, ref, here.to_x), mail.send(ref, ref, here.to_y)]
+
+    for copy in get_attn:
+        copy.wait()
+    attn_moves = set_out(0)
+    own_rows = pl.ds(pl.multiple_of(own_at, 32), share)
+    attn_peak = peak(ea[own_rows, :])
+    piece = small_src.shape[1]
+    n_pieces = n_attn // piece
+    small_src[...] = gains[...].astype(F32)
+    for index in range(n_pieces):
+        at = slice(index * piece, (index + 1) * piece)
+        small_src[index : index + 1, :] = attn_peak[:, at]
+    first = mail.send(small_src, small_land.at[0], here.to_core)
+    swap = [
+        mail.send(w.at[:, their_cols], wf_other.at[:, part_cols[i]], here.to_core)
+        for i, w in enumerate(weights)
+    ]
+    own = slab(ea, x, core, y)
+    ac = mail.send(own, own, here.to_core)
+    cot_copy = mail.send(cot_in, cots.at[pl.ds(rows, rows)], here.to_core)
+    first.wait_recv()
+
+    def merge(mine, other):
+        mine[0:8, :] = jnp.maximum(mine[0:8, :], other[0:8, :])
+        mine[8:, :] = mine[8:, :] + other[8:, :]
+
+    small[...] = small_src[...]
+    merge(small, small_land.at[0])
+    ring = (here.to_x, here.to_y, here.to_xy)
+    small_send = [mail.send(small, small_land.at[1 + i], to) for i, to in enumerate(ring)]
+
+    for copy in get_ffn:
+        copy.wait()
+    for copy in swap:
+        copy.wait_recv()
+    peaks_src[...] = jnp.zeros_like(peaks_src)
+    for part in range(3):
+        cols = slice(part * half, (part + 1) * half)
+        both = jnp.maximum(peak(wf_mine[:, cols]), peak(wf_other[:, cols]))
+        line_at = (part + 2) % 3
+        peaks_src[line_at : line_at + 1, :] = both
+    peaks_send = [mail.send(peaks_src, peaks_land.at[i], to) for i, to in enumerate(ring)]
+    attn_moves += set_out(half_share)
+
+    for copy in small_send:
+        copy.wait_recv()
+        mail.finish(copy)
+    for index in (1, 2, 3):
+        merge(small, small_land.at[index])
+    outs = [fetch(small, small_out)]
+
+    get_tokens.wait()
+    gain_one = row_of(small, 8, width // piece)
+    gain_two = row_of(small, 8 + width // piece, width // piece)
+
+    @pl.loop(0, rows // 32)
+    def _(index):
+        at = pl.ds(mul(index, 32), 32)
+        h1[at, :] = (forward_norm(tokens[at, :].astype(F32))[0] * gain_one).astype(BF16)
+
+
+    def tangent(block, bound):
+        return jnp.tanh(block.astype(F32) / bound)
+
+    for copy in peaks_send:
+        copy.wait_recv()
+    peaks[...] = peaks_src[...]
+    for index in range(3):
+        peaks[...] = jnp.maximum(peaks[...], peaks_land[index])
+    peer_copy = mail.send(peaks, peaks_peer, here.to_core)
+    outs.append(fetch(peaks, peaks_out.at[:, mine_cols]))
+    picks = (6, 4, 5)
+    other_at = here.slot(x, 1 - core, y) * share
+    for part in range(3):
+        cols = slice(part * half, (part + 1) * half)
+        line_at = (part + 2) % 3
+        bound = peaks[line_at : line_at + 1, :] * level(width_pick[picks[part]])
+
+        @pl.loop(0, share // 32)
+        def _(index, cols=cols, bound=bound, part=part):
+            at = pl.ds(mul(index, 32), 32)
+            for weight, start in ((wf_mine, own_at), (wf_other, other_at)):
+                to = pl.ds(pl.multiple_of(start + index * 32, 32), 32)
+                bent = tangent(weight[at, cols], bound)
+                effective[part][to, :] = (bound * bent).astype(BF16)
+                weight[at, cols] = (1.0 - bent * bent).astype(BF16)
+
+    outs.append(fetch(wf_mine, slope_ffn_out.at[core]))
+    outs.append(fetch(wf_other, slope_ffn_out.at[1 - core]))
+
+    for copy in attn_moves:
+        copy.wait_recv()
+    from_x = slab(ea, 1 - x, core, y)
+    corner = slab(ea, 1 - x, core, y, 0, half_share)
+    dy = mail.send(corner, corner, here.to_y)
+    cx = mail.send(from_x, from_x, here.to_core)
+    from_y = slab(ea, x, core, 1 - y)
+    corner = slab(ea, x, core, 1 - y, half_share, half_share)
+    dx = mail.send(corner, corner, here.to_x)
+    cy = mail.send(from_y, from_y, here.to_core)
+
+    splits = [pl.ds(a, b - a) for a, b in zip(cuts, cuts[1:])]
+    moving, together = {}, {}
+
+    def block_of(part, split, count):
+        return effective[part].at[pl.ds(0, count * share), splits[split]]
+
+    def move(part, split, pair, axis, ref, target):
+        if (part, split) not in together:
+            leaving, coming = block_of(part, split, 6), block_of(part, split, 4)
+            together[part, split] = mail.group(leaving, coming, here.to_x)
+        send_at, recv_at, _ = together[part, split]
+        copy = mail.send(ref, ref, target, send_at, None if pair == axis else recv_at)
+        if pair == axis:
+            moving[part, split, pair] = copy
+
+    def ship(part, split, axis, pairs=(0, 1)):
+        target = here.to_x if axis == 0 else here.to_y
+        for pair in pairs:
+            ref = slab(effective[part], x, pair, y, cols=splits[split])
+            move(part, split, pair, axis, ref, target)
+
+    def pass_on(part, split, pair):
+        moving[part, split, pair].wait_recv()
+        at = (1 - x, y) if pair == 0 else (x, 1 - y)
+        ref = slab(effective[part], at[0], pair, at[1], cols=splits[split])
+        move(part, split, pair, 2, ref, here.to_y if pair == 0 else here.to_x)
+
+    def arrived(part, split):
+        together[part, split][2].wait_recv()
+
+    ship(0, 0, 0)
+    ship(0, 0, 1, (0,))
+
+    flat_peak = row_of(small, 0, n_pieces)
+    bound_attn = jnp.concatenate(
+        [
+            flat_peak[:, :n_query] * level(width_pick[0]),
+            flat_peak[:, n_query : n_query + n_key] * level(width_pick[1]),
+            flat_peak[:, n_query + n_key : n_in] * level(width_pick[2]),
+            flat_peak[:, n_in:] * level(width_pick[3]),
+        ],
+        axis=1,
+    )
+
+    def soften(sx, score, sy, slopes=False):
+        base = here.slot(sx, score, sy) * share
+
+        @pl.loop(0, share // 32)
+        def _(index):
+            at = pl.ds(mul(index, 32), 32)
+            to = pl.ds(pl.multiple_of(base + index * 32, 32), 32)
+            bent = tangent(ea[to, :], bound_attn)
+            ea[to, :] = (bound_attn * bent).astype(BF16)
+            if slopes:
+                slope_attn[at, :] = (1.0 - bent * bent).astype(BF16)
+
+    for copy in attn_moves + [ac]:
+        mail.finish(copy)
+    soften(x, core, y, True)
+    outs.append(fetch(slope_attn, slope_attn_out))
+    ac.wait_recv()
+    soften(x, 1 - core, y)
+    cx.wait_recv()
+    soften(1 - x, 1 - core, y)
+    cy.wait_recv()
+    soften(x, 1 - core, 1 - y)
+    dy.wait_recv()
+    dx.wait_recv()
+    across = slab(ea, 1 - x, core, 1 - y)
+    cxy = mail.send(across, across, here.to_core)
+    for copy in (dy, cx, dx, cy):
+        mail.finish(copy)
+    soften(1 - x, core, y)
+    soften(x, core, 1 - y)
+    cxy.wait_recv()
+    mail.finish(cxy)
+    soften(1 - x, core, 1 - y)
+    soften(1 - x, 1 - core, 1 - y)
+    e_attn_copy = fetch(ea, e_attn_out)
+
+    tile = 256
+
+    @pl.loop(0, n_query // tile)
+    def _(index):
+        cols = pl.ds(mul(index, tile), tile)
+        query[:rows, cols] = natural(h1[...], ea[:, cols]).astype(BF16)
+
+    @pl.loop(0, 2 * n_key // tile)
+    def _(index):
+        cols = pl.ds(mul(index, tile), tile)
+        source = pl.ds(pl.multiple_of(n_query + index * tile, tile), tile)
+        kv[:rows, cols] = natural(h1[...], ea[:, source]).astype(BF16)
+
+    ours, theirs = pl.ds(edge(y, rows), EXTRA), pl.ds(rows, EXTRA)
+    row_copies = [
+        mail.send(ref.at[ours], ref.at[theirs], here.to_y) for ref in (query, kv)
+    ]
+    for part in (1, 2):
+        ship(part, 0, 0)
+    h1_copy = fetch(h1, h1_out)
+    number_rows(segments, y, keys)
+    for copy in row_copies:
+        copy.wait_recv()
+
+    block, n_heads = 128, n_query // HD
+
+    def attend(at, allowed):
+        stack = jnp.concatenate([query[at, i * HD : (i + 1) * HD] for i in range(n_heads)], axis=0)
+        probs, _ = soft_probs(stack, kv, allowed)
+        return inner_rows(probs.astype(BF16), kv[:, HD:]).astype(BF16)
+
+    out = attend(theirs, extra_visible(keys, y, n_heads))
+    for i in range(n_heads):
+        extra_heads[:, i * HD : (i + 1) * HD] = out[i * EXTRA : (i + 1) * EXTRA]
+    extra_copy = mail.send(extra_heads, extra_land, here.to_y)
+    ship(0, 0, 1, (1,))
+    for part in (1, 2):
+        ship(part, 0, 1)
+
+    @pl.loop(0, rows // block)
+    def _(index):
+        at = pl.ds(mul(index, block), block)
+        start = pl.multiple_of(y * rows + index * block, block)
+        numbers = segments[:, pl.ds(start, block)].astype(F32)
+        position = start + lax.broadcasted_iota(jnp.int32, (1, block), 1)
+        allowed = visible(keys, beside(numbers, n_heads), beside(position, n_heads), y)
+        out = attend(at, allowed)
+        for i in range(n_heads):
+            heads[at, i * HD : (i + 1) * HD] = out[i * block : (i + 1) * block]
+
+    extra_copy.wait_recv()
+    middle = (lax.broadcasted_iota(jnp.int32, (EXTRA, 1), 0) == 0) & (y == 1)
+    heads[:EXTRA, :] = jnp.where(middle, extra_land[...], heads[:EXTRA, :])
+
+    @pl.loop(0, width // tile)
+    def _(index):
+        cols = pl.ds(mul(index, tile), tile)
+        partial[:, cols] = against(heads[...], ea[cols, n_in:]).astype(BF16)
+
+    outs += [fetch(query, query_out), fetch(kv, kv_out), fetch(heads, heads_out)]
+
+    tall = 512
+
+    def back_into_mixed(split):
+        @pl.loop(0, 2 * rows // tall)
+        def _(index):
+            at = pl.ds(mul(index, tall), tall)
+            grad_gate[at, splits[split]] = natural(cots[at, :], ed[:, splits[split]]).astype(BF16)
+
+    def gated(split):
+        cols, high = splits[split], 512 if split else 256
+
+        @pl.loop(0, 2 * rows // high)
+        def _(index):
+            at = pl.ds(mul(index, high), high)
+            gate = natural(h2[at, :], eg[:, cols])
+            upper = natural(h2[at, :], eu[:, cols])
+            value, slope = gelu_pair(gate)
+            back = grad_gate[at, cols].astype(F32)
+            mixed_in[at, cols] = (value * upper).astype(BF16)
+            grad_gate[at, cols] = (back * upper * slope).astype(BF16)
+            grad_up[at, cols] = (back * value).astype(BF16)
+
+    def to_width(target, pairs, split, then=None):
+        wide = width // 3
+
+        def piece(at):
+            for column in range(3):
+                cols = slice(column * wide, (column + 1) * wide)
+                added = against(pairs[0][0][at, splits[split]], pairs[0][1][cols, splits[split]])
+                for left, right in pairs[1:]:
+                    added += against(left[at, splits[split]], right[cols, splits[split]])
+                if split:
+                    added += target[column][at, :].astype(F32)
+                target[column][at, :] = added.astype(BF16)
+
+        if then is None:
+
+            @pl.loop(0, 2 * rows // tall)
+            def _(index):
+                piece(pl.ds(mul(index, tall), tall))
+
+        else:
+            for first in range(0, 2 * rows, tall):
+                piece(pl.ds(first, tall))
+                then(pl.ds(first, tall))
+
+    def transform(sub, spot, summed):
+        at = pl.ds(pl.multiple_of(z * (rows // 4) + sub * line.part, line.part), line.part)
+        resid = tokens[at, :].astype(F32) + summed
+        x1[spot, :] = resid
+        return (forward_norm(resid)[0] * gain_two).astype(BF16)
+
+    own_half, other_half = (h2.at[pl.ds(first, rows)] for first in (0, rows))
+    give_send, give_recv, all_given = mail.group(own_half, other_half, here.to_core)
+
+    def give(sub):
+        for chunk in range(4):
+            first = chunk * (rows // 4) + sub * line.part
+            src, dst = (h2.at[pl.ds(first + at, line.part)] for at in (0, rows))
+            mail.send(src, dst, here.to_core, give_send, give_recv)
+
+    line = Line(here, partial, h2, land, total, (line_send, line_recv), transform, give=give, subs=FRONT_SUBS)
+    width_blocks = [pl.ds(i * (width // 3), width // 3) for i in range(3)]
+    back_part = [rows_a.at[:, cols] for cols in width_blocks]
+    spare = ((0, 0), (0, 1), (1, 0))
+    ffn_part = [
+        ea.at[pl.ds(i * 2 * rows, 2 * rows), pl.ds(j * (width // 3), width // 3)] for i, j in spare
+    ]
+    upward = ((grad_gate, eg), (grad_up, eu))
+    downward = ((mixed_in, ed),)
+    for tick in line.ticks():
+        if tick == 1:
+            pass_on(0, 0, 0)
+            pass_on(0, 0, 1)
+        if tick == 2:
+            pass_on(1, 0, 0)
+        if tick == 3:
+            get_cot.wait()
+            cot_copy.wait_recv()
+            cot_keep = fetch(cots.at[pl.ds(rows, rows)], cot_out)
+        if tick == 4:
+            pass_on(1, 0, 1)
+            pass_on(2, 0, 0)
+        if tick == 5:
+            pass_on(2, 0, 1)
+            for part in range(3):
+                for axis in (0, 1):
+                    ship(part, 1, axis)
+        if tick == 8:
+            for axis in (0, 1):
+                ship(0, 2, axis)
+        if tick == 6:
+            arrived(0, 0)
+            back_into_mixed(0)
+    line.close()
+    outs.append(fetch(x1, x1_out))
+    arrived(1, 0)
+    arrived(2, 0)
+    all_given.wait_recv()
+    outs.append(fetch(h2, h2_out))
+    gated(0)
+    for part in range(3):
+        for turn in (0, 1):
+            pass_on(part, 1, turn)
+    for part in (1, 2):
+        for axis in (0, 1):
+            ship(part, 2, axis)
+    h1_copy.wait()
+    to_width(back_part, upward, 0)
+    arrived(0, 1)
+    back_into_mixed(1)
+    arrived(1, 1)
+    arrived(2, 1)
+    gated(1)
+    e_attn_copy.wait()
+    to_width(ffn_part, downward, 0)
+    to_width(back_part, upward, 1)
+    to_width(ffn_part, downward, 1)
+    for part in range(3):
+        for turn in (0, 1):
+            pass_on(part, 2, turn)
+    late = cuts[2]
+
+    def early_copy(index):
+        at = pl.ds(mul(index, tile), tile)
+        return pltpu.make_async_copy(early_made, early_out.at[at], early_sem)
+
+    @pl.loop(0, width // tile)
+    def _(index):
+        made = inner_rows(h2[:, pl.ds(mul(index, tile), tile)], grad_gate[:, :late]).astype(BF16)
+
+        @pl.when(index > 0)
+        def _():
+            early_copy(index - 1).wait()
+
+        early_made[...] = made
+        early_copy(index).start()
+
+    early_copy(width // tile - 1).wait()
+    arrived(0, 2)
+    back_into_mixed(2)
+    arrived(1, 2)
+    arrived(2, 2)
+    gated(2)
+    outs += [
+        fetch(mixed_in, mixed_in_out),
+        fetch(grad_gate, grad_gate_out),
+        fetch(grad_up, grad_up_out),
+    ]
+    to_width(back_part, upward, 2, lambda at: outs.append(fetch(rows_a.at[at], back_out.at[at])))
+
+    def ffn_leaves(at):
+        for i in range(3):
+            outs.append(fetch(ffn_part[i].at[at], ffn_out.at[at, width_blocks[i]]))
+
+    to_width(ffn_part, downward, 2, ffn_leaves)
+    cot_keep.wait()
+    peer_copy.wait_recv()
+    outs.append(fetch(peaks_peer, peaks_out.at[:, their_cols]))
+    mail.close()
+    for copy in outs:
+        copy.wait()
+
+
+def front(width_pick, weights, gains, tokens, cotangent, segments):
+    rows, width = tokens.shape
+    share, n_query = weights[0].shape
+    n_kv = 2 * weights[1].shape[1]
+    n_attn = 2 * n_query + n_kv
+    hidden = weights[-1].shape[1]
+    half = hidden // 2
+    shapes = [
+        ((width, n_attn), BF16),
+        ((2 * rows, width), BF16),
+        ((rows // 4, width), F32),
+        ((rows + EXTRA, n_query), BF16),
+        ((rows + EXTRA, n_kv), BF16),
+        ((rows, n_query), BF16),
+        ((rows, width), BF16),
+        ((rows, width), BF16),
+        ((2 * rows, half), BF16),
+        ((2 * rows, half), BF16),
+        ((2 * rows, half), BF16),
+        ((2 * rows, width), BF16),
+        ((2 * rows, width), BF16),
+        ((2, share, 3 * half), BF16),
+        ((share, n_attn), BF16),
+        ((32, 256), F32),
+        ((8, hidden), F32),
+        ((width, 7 * half // 9), BF16),
+    ]
+    in_vmem = pl.BlockSpec(memory_space=pltpu.VMEM)
+    in_smem = pl.BlockSpec(memory_space=pltpu.SMEM)
+    anywhere = pl.BlockSpec(memory_space=pl.ANY)
+    scratch = [
+        pltpu.VMEM((share, 3 * half), BF16),
+        pltpu.VMEM((share, 3 * half), BF16),
+        pltpu.VMEM((width, n_attn), BF16),
+        pltpu.VMEM((width, half), BF16),
+        pltpu.VMEM((width, half), BF16),
+        pltpu.VMEM((width, half), BF16),
+        pltpu.VMEM((2 * rows, width), BF16),
+        pltpu.VMEM((2 * rows, width), BF16),
+        pltpu.VMEM((rows + EXTRA, n_query), BF16),
+        pltpu.VMEM((rows + EXTRA, n_kv), BF16),
+        pltpu.VMEM((rows, n_query), BF16),
+        pltpu.VMEM((2 * rows, width), BF16),
+        pltpu.VMEM((rows // 4, width), F32),
+        pltpu.VMEM((2 * rows, half), BF16),
+        pltpu.VMEM((2 * rows, half), BF16),
+        pltpu.VMEM((2 * rows, half), BF16),
+        pltpu.VMEM((share, n_attn), BF16),
+        pltpu.VMEM((32, 256), F32),
+        pltpu.VMEM((4, 32, 256), F32),
+        pltpu.VMEM((32, 256), F32),
+        pltpu.VMEM((8, half), F32),
+        pltpu.VMEM((3, 8, half), F32),
+        pltpu.VMEM((8, half), F32),
+        pltpu.VMEM((8, half), F32),
+        pltpu.VMEM((rows + EXTRA, 128), F32),
+        pltpu.VMEM((EXTRA, n_query), BF16),
+        pltpu.VMEM((EXTRA, n_query), BF16),
+        pltpu.VMEM((256, 7 * half // 9), BF16),
+        pltpu.SemaphoreType.DMA,
+        *line_scratch(rows, width, FRONT_SUBS),
+        pltpu.SemaphoreType.DMA((34,)),
+        pltpu.SemaphoreType.DMA((35,)),
+        pltpu.SemaphoreType.DMA((53,)),
+    ]
+    return pl.pallas_call(
+        front_kernel,
+        out_shape=[jax.ShapeDtypeStruct(s, d) for s, d in shapes],
+        in_specs=[in_smem] + [anywhere] * 7 + [in_vmem, anywhere, anywhere, in_vmem],
+        out_specs=[anywhere] * len(shapes),
+        scratch_shapes=scratch,
+        compiler_params=pltpu.CompilerParams(
+            collective_id=0, has_side_effects=True, vmem_limit_bytes=VMEM_BYTES
+        ),
+        cost_estimate=pl.CostEstimate(
+            flops=36 * 10**9, bytes_accessed=90 * 10**6, transcendentals=8 * 10**6
+        ),
+        name="front",
+    )(width_pick, *weights, gains, tokens, cotangent, segments)
+
+
+OUTPUT_PLAN = (7, 8, 10, 11, 12, 14, 15, 17, 18, 19, 20, 21, 22, 23)
+
+
+def back_kernel(
+    back_in,
+    ffn_in,
+    mixed_in,
+    grad_gate,
+    grad_up,
+    h2_in,
+    cot_other,
+    early_in,
+    x1_in,
+    small,
+    e_attn,
+    query_in,
+    kv_in,
+    heads_in,
+    h1_in,
+    tokens_in,
+    cot_in,
+    segments,
+    slope_ffn,
+    slope_attn_in,
+    out_down,
+    out_gate,
+    out_up,
+    out_attn,
+    mixed_out,
+    tokens_out,
+    gains_out,
+    de_down,
+    de_gate,
+    de_up,
+    stage_a,
+    stage_b,
+    land_a,
+    land_b,
+    last_a,
+    last_b,
+    slopes,
+    partial,
+    partial_ffn,
+    grad_resid_b,
+    own_ffn,
+    own_tokens,
+    land,
+    land_ffn,
+    total,
+    ea,
+    core_land,
+    attn_a,
+    attn_b,
+    attn_last_a,
+    attn_last_b,
+    query,
+    kv,
+    heads,
+    h1,
+    keys,
+    grad_in,
+    grad_kv,
+    edge_send,
+    edge_land,
+    row_send,
+    row_land,
+    x1,
+    grad_resid,
+    token_chunk,
+    cot_chunk,
+    gain_part,
+    gain_sum,
+    gain_land,
+    line_send,
+    line_recv,
+    ffn_send,
+    ffn_recv,
+    work_sem,
+    local_sem,
+    send_sem,
+    recv_sem,
+):
+    here = Place()
+    x, y, z, core = here.x, here.y, here.z, here.core
+    rows, width = tokens_in.shape
+    share, half = last_a.shape[1], last_a.shape[2]
+    n_query, n_attn = query.shape[1], ea.shape[1]
+    n_in = n_attn - n_query
+    de_ffn = (de_down, de_gate, de_up)
+    out_ffn = (out_down, out_gate, out_up)
+    chunk_rows = pl.ds(pl.multiple_of(z * (rows // 4), rows // 4), rows // 4)
+    mine_cols = pl.ds(pl.multiple_of(core * half, half), half)
+    tile = 256
+
+    local_count = [0]
+
+    def fetch(src, dst):
+        copy = pltpu.make_async_copy(src, dst, local_sem.at[local_count[0]])
+        local_count[0] += 1
+        copy.start()
+        return copy
+
+    order = (1, 2, 0)
+    slot_of = {part: i % 2 for i, part in enumerate(order)}
+
+    late = early_in.shape[1]
+    blocks = {0: [(de_down, 0, half)], 2: [(de_up, 0, half)]}
+    blocks[1] = [(early_in, 0, late), (de_gate, late, half - late)]
+
+    def lanes(ref, block):
+        return ref if ref.shape[-1] == block[2] else ref.at[:, pl.ds(block[1], block[2])]
+
+    def source(block, at):
+        return lanes(block[0].at[at], block)
+
+    def stage(part):
+        a_rows = pl.ds(pl.multiple_of(here.slot(x, 0, 0) * share, share), 2 * share)
+        slot = slot_of[part]
+        copies = []
+        for block in blocks[part]:
+            copies.append(fetch(source(block, a_rows), lanes(stage_a.at[slot], block)))
+            for i in (0, 1):
+                b_rows = pl.ds(mul(here.slot(i, 1, y), share), share)
+                copies.append(fetch(source(block, b_rows), lanes(stage_b.at[slot, i], block)))
+        return copies
+
+    sides = (mixed_in, grad_gate, grad_up)
+    side_rows = [pl.ds(0, 2 * rows), pl.ds(2 * rows, 2 * rows), pl.ds(0, 2 * rows)]
+    side_at = {part: ea.at[side_rows[i], pl.ds(0, half)] for i, part in enumerate(order)}
+    strip_cols = pl.ds(half, tile)
+    made_cols = {part: pl.ds(blocks[part][-1][1], blocks[part][-1][2]) for part in order}
+
+    def strip_copies(part, index, slot):
+        cols = pl.ds(mul(index, tile), tile)
+        to = [
+            ea.at[pl.ds(pl.multiple_of(slot * 2 * rows + i * rows, rows), rows), strip_cols]
+            for i in (0, 1)
+        ]
+        if part:
+            src = [h2_in.at[pl.ds(i * rows, rows), cols] for i in (0, 1)]
+        else:
+            src = [cot_in.at[:, cols], cot_other.at[:, cols]]
+        return [
+            pltpu.make_async_copy(src[i], to[i], work_sem.at[slot, i]) for i in (0, 1)
+        ]
+
+    def result_copy(part, index):
+        at = pl.ds(mul(index, tile), tile)
+        cols = made_cols[part]
+        slot = lax.rem(index, 2)
+        made = slopes.at[slot, pl.ds(0, tile), cols]
+        return pltpu.make_async_copy(made, de_ffn[part].at[at, cols], work_sem.at[2, slot])
+
+    sides_here = {order[0]: fetch(sides[order[0]], side_at[order[0]])}
+    for copy in strip_copies(order[0], 0, 0):
+        copy.start()
+    get_x1 = fetch(x1_in, x1)
+    get_cot = fetch(cot_in.at[chunk_rows], cot_chunk)
+    get_tokens = fetch(tokens_in.at[chunk_rows], token_chunk)
+    get_partial = fetch(back_in.at[pl.ds(0, rows)], partial)
+    sides_here[order[1]] = fetch(sides[order[1]], side_at[order[1]])
+    far_target = (x * 2 + core, y, lax.rem(z + 2, 4))
+    near_target = (x * 2 + core, y, z + 1 - 2 * lax.rem(z, 2))
+    plane = [here.to_core, here.to_x, here.to_y, here.to_xy]
+    plane += [(2 * (1 - x) + 1 - core, y, z), (2 * x + 1 - core, 1 - y, z)]
+    plane += [(2 * (1 - x) + 1 - core, 1 - y, z)]
+    greet(here, [*plane, far_target])
+    mail = Mail(send_sem, recv_sem)
+    their_half = pl.ds(rows, rows)
+    chunks = [jnp.where(z < 2, 3 - i, i) * (rows // 4) for i in range(4)]
+    chunks = [pl.multiple_of(first, rows // 4) for first in chunks]
+    back_copies = [
+        mail.send(
+            back_in.at[pl.ds(rows + first, rows // 4)],
+            partial_ffn.at[pl.ds(first, rows // 4)],
+            here.to_core,
+        )
+        for first in chunks
+    ]
+    ffn_copy = mail.send(ffn_in.at[their_half], h1, here.to_core)
+
+    n_strips = width // tile
+
+    def strips(part, first, last):
+        if first == 0:
+            sides_here[part].wait()
+
+        @pl.loop(first, last)
+        def _(index):
+            slot = lax.rem(index, 2)
+            for copy in strip_copies(part, index, slot):
+                copy.wait()
+
+            @pl.when(index + 1 < n_strips)
+            def _():
+                for copy in strip_copies(part, index + 1, 1 - slot):
+                    copy.start()
+
+            left = ea[pl.ds(pl.multiple_of(slot * 2 * rows, rows), 2 * rows), strip_cols]
+            made = inner_rows(left, side_at[part][:, made_cols[part]]).astype(BF16)
+
+            @pl.when(index > 1)
+            def _():
+                result_copy(part, index - 2).wait()
+
+            slopes[slot, :tile, made_cols[part]] = made
+            result_copy(part, index).start()
+
+        if last == n_strips:
+            for index in (n_strips - 2, n_strips - 1):
+                result_copy(part, jnp.int32(index)).wait()
+            at = order.index(part)
+            if at + 1 < 3:
+                for copy in strip_copies(order[at + 1], 0, 0):
+                    copy.start()
+            if at == 0:
+                sides_here[order[2]] = fetch(sides[order[2]], side_at[order[2]])
+            if at < 2:
+                staged[part] = stage(part)
+
+    staged = {}
+    slope_here = {}
+
+    def get_slopes(part):
+        cols = pl.ds(part * half, half)
+        slope_here[part] = fetch(slope_ffn.at[:, :, cols], slopes)
+
+    first_hop, groups = {}, {}
+    second_hop = {}
+    ending = []
+
+    def ship(part, i, block, axis):
+        if axis == 0:
+            at = pl.ds(mul(here.slot(1 - x, 0, i), share), share)
+            to, target = land_a.at[part, pl.ds(i * share, share)], here.to_x
+        else:
+            at = pl.ds(mul(here.slot(i, 1, 1 - y), share), share)
+            to, target = land_b.at[part, i], here.to_y
+        if (part, block[1]) not in groups:
+            four = lanes(de_ffn[part].at[pl.ds(0, 4 * share)], block)
+            groups[part, block[1]] = mail.group(four, four, here.to_x)
+            first_hop.setdefault(part, []).append(groups[part, block[1]][2])
+        mail.send(source(block, at), lanes(to, block), target, *groups[part, block[1]][:2])
+
+    def ship_all(part, i, axes=(0, 1)):
+        for block in blocks[part]:
+            for axis in axes:
+                ship(part, i, block, axis)
+
+    step = 32
+
+    def relay(part):
+        slot = slot_of[part]
+        for copy in staged[part]:
+            copy.wait()
+        for copy in first_hop[part]:
+            copy.wait_recv()
+        base = (1 - y) * share
+
+        @pl.loop(0, share // step)
+        def _(index):
+            at = pl.ds(pl.multiple_of(base + index * step, step), step)
+            mine = stage_a[slot, at, :].astype(F32) + land_a[part, at, :].astype(F32)
+            stage_a[slot, at, :] = mine.astype(BF16)
+            at = pl.ds(mul(index, step), step)
+            mine = stage_b[slot, 1 - x, at, :].astype(F32) + land_b[part, 1 - x, at, :].astype(F32)
+            stage_b[slot, 1 - x, at, :] = mine.astype(BF16)
+
+        a_src = stage_a.at[slot, pl.ds(pl.multiple_of(base, share), share)]
+        second_hop[part] = (
+            mail.send(a_src, last_a.at[part], here.to_y),
+            mail.send(stage_b.at[slot, 1 - x], last_b.at[part], here.to_x),
+        )
+
+    def settle(part):
+        slot = slot_of[part]
+        slope_here[part].wait()
+        for copy in second_hop[part]:
+            copy.wait_recv()
+        base = y * share
+
+        @pl.loop(0, share // step)
+        def _(index):
+            flat = pl.ds(mul(index, step), step)
+            at = pl.ds(pl.multiple_of(base + index * step, step), step)
+            mine = stage_a[slot, at, :].astype(F32) + land_a[part, at, :].astype(F32)
+            mine = mine + last_a[part, flat, :].astype(F32)
+            stage_a[slot, at, :] = (mine * slopes[0, flat, :].astype(F32)).astype(BF16)
+            mine = stage_b[slot, x, flat, :].astype(F32) + land_b[part, x, flat, :].astype(F32)
+            mine = mine + last_b[part, flat, :].astype(F32)
+            stage_b[slot, x, flat, :] = (mine * slopes[1, flat, :].astype(F32)).astype(BF16)
+
+        a_ref = stage_a.at[slot, pl.ds(pl.multiple_of(base, share), share)]
+        b_ref = stage_b.at[slot, x]
+        out = out_ffn[part].at[:, mine_cols]
+        give_b = mail.make(b_ref, out, here.to_core)
+        give_a = mail.make(a_ref, out, here.to_core, mail.n_send - 1, mail.n_recv - 1)
+        keep_a = pltpu.make_async_copy(a_ref, out, local_sem.at[local_count[0]])
+        keep_b = pltpu.make_async_copy(b_ref, out, local_sem.at[local_count[0]])
+        local_count[0] += 1
+
+        @pl.when(core == 0)
+        def _():
+            keep_a.start()
+            give_b.start()
+
+        @pl.when(core == 1)
+        def _():
+            keep_b.start()
+            give_a.start()
+
+        ending.append((keep_a, give_b))
+        finished[part] = ending[-1]
+
+    finished = {}
+
+    def restage(part, earlier):
+        keep, give = finished[earlier]
+        keep.wait()
+        for copy in (give, *second_hop[earlier]):
+            mail.finish(copy)
+        staged[part] = stage(part)
+
+    count = width // small.shape[1]
+    gain_one = row_of(small, 8, count)
+    gain_two = row_of(small, 8 + count, count)
+
+    gain_part[...] = jnp.zeros_like(gain_part)
+
+    def into_resid(sub, spot, summed):
+        normed, inverse = forward_norm(x1[spot, :])
+        gain_part[1:2, :] += jnp.sum(summed * normed, axis=0, keepdims=True)
+        grad = cot_chunk[spot, :].astype(F32) + backward_norm(summed * gain_two, normed, inverse)
+        grad_resid[spot, :] = grad
+        return grad.astype(BF16)
+
+    def into_mixed(sub, spot, summed):
+        return (x1[spot, :] + summed).astype(BF16)
+
+    def into_tokens(sub, spot, summed):
+        normed, inverse = forward_norm(token_chunk[spot, :].astype(F32))
+        gain_part[0:1, :] += jnp.sum(summed * normed, axis=0, keepdims=True)
+        grad = grad_resid[spot, :] + backward_norm(summed * gain_one, normed, inverse)
+        return grad.astype(BF16)
+
+    line = Line(here, partial, grad_resid_b, land, total, (line_send, line_recv), into_resid, subs=BACK_SUBS)
+    ffn_line = Line(
+        here, partial_ffn, mixed_out, land_ffn, total, (ffn_send, ffn_recv), into_mixed, own_ffn, subs=BACK_SUBS
+    )
+    tok_line = Line(
+        here, partial, tokens_out, land, total, (line_send, line_recv), into_tokens, own_tokens, subs=BACK_SUBS
+    )
+
+    for i in (0, 1):
+        for axis in (0, 1):
+            ship(1, i, blocks[1][0], axis)
+    for copy in (get_partial, get_x1, get_cot, get_tokens):
+        copy.wait()
+
+    def join(target, came, first=0, count=rows):
+        @pl.loop(0, count // step)
+        def _(index):
+            at = pl.ds(pl.multiple_of(first + index * step, step), step)
+            target[at, :] = (target[at, :].astype(F32) + came[at, :].astype(F32)).astype(BF16)
+
+    def join_chunk(number):
+        back_copies[number].wait_recv()
+        join(partial, partial_ffn, chunks[number], rows // 4)
+
+    join_chunk(0)
+
+    quarter, n_heads = 32, n_query // HD
+    block = 4 * quarter
+    number_rows(segments, y, keys)
+    grad_kv[...] = jnp.zeros_like(grad_kv)
+
+    def stacked(value):
+        return jnp.concatenate([value[:, i * HD : (i + 1) * HD] for i in range(n_heads)], axis=0)
+
+    def back_through(query_b, grad_o, allowed):
+        probs, bent = soft_probs(query_b, kv, allowed)
+        grad_probs = against(kv[:, HD:], grad_o)
+        row_dot = jnp.sum(probs * grad_probs, axis=0, keepdims=True)
+        grad_raw = probs * (grad_probs - row_dot) * (1.0 - bent * bent) * HD ** (-0.5)
+        grad_raw = grad_raw.astype(BF16)
+        grad_kv[:, :HD] += natural(grad_raw, query_b)
+        grad_kv[:, HD:] += natural(probs.astype(BF16), grad_o)
+        return inner_rows(grad_raw, kv[:, :HD]).astype(BF16)
+
+    def attend_back(sub):
+        firsts = [j * (rows // 4) + sub * quarter for j in range(4)]
+        spots = [slice(at, at + quarter) for at in firsts]
+
+        def take(ref):
+            return jnp.concatenate([ref[spot, :] for spot in spots], axis=0)
+
+        index = lax.broadcasted_iota(jnp.int32, (1, block), 1)
+        chunk = sum((index >= j * quarter).astype(jnp.int32) for j in (1, 2, 3))
+        position = y * rows + index + chunk * (rows // 4 - quarter) + sub * quarter
+        numbers = jnp.transpose(take(keys))[0:1, :]
+        allowed = visible(keys, beside(numbers, n_heads), beside(position, n_heads), y)
+        grad_o = natural(take(grad_resid_b), ea[:, n_in:]).astype(BF16)
+        if sub == 0:
+            edge_send[...] = grad_o[:EXTRA]
+            edge_copies.append(mail.send(edge_send, edge_land, here.to_y))
+            theirs = (lax.broadcasted_iota(jnp.int32, (block, 1), 0) == 0) & (y == 1)
+            grad_o = jnp.where(theirs, jnp.zeros_like(grad_o), grad_o)
+        grad_q = back_through(stacked(take(query)), stacked(grad_o), allowed)
+        for i in range(n_heads):
+            for j, spot in enumerate(spots):
+                at = i * block + j * quarter
+                grad_in[spot, i * HD : (i + 1) * HD] = grad_q[at : at + quarter]
+
+    edge_copies = []
+
+    def edge_back():
+        edge_copies[0].wait_recv()
+        ours = (lax.broadcasted_iota(jnp.int32, (EXTRA, 1), 0) == 0) & (y == 0)
+        grad_o = jnp.where(ours, edge_land[...], jnp.zeros_like(edge_land))
+        allowed = extra_visible(keys, y, n_heads)
+        grad_q = back_through(stacked(query[rows:, :]), stacked(grad_o), allowed)
+        for i in range(n_heads):
+            row_send[:, i * HD : (i + 1) * HD] = grad_q[i * EXTRA : (i + 1) * EXTRA]
+        row_send[:, n_query:] = grad_kv[rows:, :].astype(BF16)
+
+    ffn_ticks = ffn_line.ticks()
+    plan, count = list(OUTPUT_PLAN), itertools.count(2)
+
+    def output_wave(place):
+        while plan and plan[0] <= place:
+            plan.pop(0)
+            next(ffn_ticks, None)
+
+    later = []
+    for tick in line.ticks():
+        if tick == 0:
+            join_chunk(1)
+        if tick == 1:
+            join_chunk(2)
+            join_chunk(3)
+            get_ffn = fetch(ffn_in.at[pl.ds(0, rows)], partial_ffn)
+            strips(1, 0, n_strips // 2)
+        if tick == 2:
+            strips(1, n_strips // 2, n_strips)
+            for i in (0, 1):
+                for axis in (0, 1):
+                    ship(1, i, blocks[1][1], axis)
+        if tick in (3, 4, 5):
+            strips(2, 3 * tick - 9, 3 * tick - 6)
+        if tick == 5:
+            ship_all(2, 0)
+            ship_all(2, 1)
+        if tick in (6, 7):
+            strips(0, 5 * tick - 30, min(5 * tick - 25, n_strips))
+        if tick == 5:
+            get_ffn.wait()
+            ffn_copy.wait_recv()
+            join(partial_ffn, h1)
+            get_h1 = fetch(h1_in, h1)
+        if tick == 7:
+            later = [
+                fetch(e_attn, ea),
+                fetch(query_in, query),
+                fetch(kv_in, kv),
+                fetch(heads_in, heads),
+            ]
+        output_wave(tick)
+        if tick == 9:
+            get_slopes(1)
+            relay(1)
+        if tick == 11:
+            ship_all(0, 0, (0,))
+        if tick == 8:
+            for copy in later:
+                copy.wait()
+        if tick in (8, 10, 12, 13):
+            attend_back((8, 10, 12, 13).index(tick))
+    output_wave(14)
+    line.close()
+    edge_back()
+    row_copy = mail.send(row_send, row_land, here.to_y)
+    ship_all(0, 0, (1,))
+    ship_all(0, 1)
+    output_wave(15)
+    settle(1)
+    get_slopes(2)
+    restage(0, 1)
+    row_copy.wait_recv()
+    at = pl.ds(edge(y, rows), EXTRA)
+    grad_in[at, :n_query] = (grad_in[at, :n_query].astype(F32) + row_land[:, :n_query].astype(F32)).astype(BF16)
+    grad_kv[at, :] += row_land[:, n_query:].astype(F32)
+    grad_in[:, n_query:] = grad_kv[:rows, :].astype(BF16)
+
+    @pl.loop(0, width // tile)
+    def _(index):
+        cols = pl.ds(mul(index, tile), tile)
+        partial[:, cols] = against(grad_in[...], ea[cols, :n_in]).astype(BF16)
+
+    tok_ticks = tok_line.ticks()
+    next(tok_ticks, None)
+    output_wave(17)
+
+    @pl.loop(0, width // tile)
+    def _(index):
+        cols = pl.ds(mul(index, tile), tile)
+        ea[cols, n_in:] = inner_rows(grad_resid_b[:, cols], heads[...]).astype(BF16)
+
+    next(tok_ticks, None)
+    output_wave(18)
+    relay(2)
+    get_h1.wait()
+
+    @pl.loop(0, width // tile)
+    def _(index):
+        cols = pl.ds(mul(index, tile), tile)
+        ea[cols, :n_in] = inner_rows(h1[:, cols], grad_in[...]).astype(BF16)
+
+    def pair_rows(sx, score):
+        return pl.ds(pl.multiple_of(here.slot(sx, score, 0) * share, 2 * share), 2 * share)
+
+    core_copies = [
+        mail.send(ea.at[pair_rows(i, 1 - core)], core_land.at[i], here.to_core) for i in (0, 1)
+    ]
+    for _ in range(2):
+        next(tok_ticks, None)
+        output_wave(17 + next(count))
+    for copy in core_copies:
+        copy.wait_recv()
+
+    @pl.loop(0, 2 * share // step)
+    def _(index):
+        for i in (0, 1):
+            at = pl.ds(
+                pl.multiple_of(here.slot(i, core, 0) * share + index * step, step), step
+            )
+            flat = pl.ds(mul(index, step), step)
+            ea[at, :] = (ea[at, :].astype(F32) + core_land[i, flat, :].astype(F32)).astype(BF16)
+
+    slope_attn = core_land.at[0, pl.ds(0, share)]
+    get_slope_attn = fetch(slope_attn_in, slope_attn)
+    cut = attn_a.shape[1]
+    left, right = pl.ds(0, cut), pl.ds(cut, n_attn - cut)
+
+    def one_rows(sx, sy):
+        return pl.ds(pl.multiple_of(here.slot(sx, core, sy) * share, share), share)
+
+    attn_first = [mail.send(ea.at[pair_rows(1 - x, core), left], attn_a, here.to_x)]
+    for i in (0, 1):
+        attn_first.append(mail.send(ea.at[one_rows(i, 1 - y), right], attn_b.at[i], here.to_y))
+    for _ in range(2):
+        next(tok_ticks, None)
+        output_wave(17 + next(count))
+    relay(0)
+    settle(2)
+    get_slopes(0)
+    for _ in range(3):
+        next(tok_ticks, None)
+        output_wave(17 + next(count))
+
+    def gain_steps():
+        rounds = (plane, [near_target], [far_target])
+        mine, at = gain_part, 0
+        for number, targets in enumerate(rounds):
+            places = gain_land.at[pl.ds(at, len(targets))]
+            send_at, recv_at, came = mail.group(places, places, here.to_core)
+            for i, target in enumerate(targets):
+                mail.send(mine, gain_land.at[at + i], target, send_at, recv_at)
+            yield
+            came.wait_recv()
+            added = mine[...]
+            for i in range(len(targets)):
+                added = added + gain_land[at + i]
+            gain_sum[number] = added
+            mine, at = gain_sum.at[number], at + len(targets)
+
+    gain_waves = gain_steps()
+    for copy in attn_first:
+        copy.wait_recv()
+
+    @pl.loop(0, share // step)
+    def _(index):
+        flat = pl.ds(mul(index, step), step)
+        at = pl.ds(pl.multiple_of(here.slot(x, core, 1 - y) * share + index * step, step), step)
+        came = pl.ds(pl.multiple_of((1 - y) * share + index * step, step), step)
+        ea[at, left] = (ea[at, left].astype(F32) + attn_a[came, :].astype(F32)).astype(BF16)
+        at = pl.ds(pl.multiple_of(here.slot(1 - x, core, y) * share + index * step, step), step)
+        ea[at, right] = (
+            ea[at, right].astype(F32) + attn_b[1 - x, flat, :].astype(F32)
+        ).astype(BF16)
+
+    attn_second = [
+        mail.send(ea.at[one_rows(x, 1 - y), left], attn_last_a, here.to_y),
+        mail.send(ea.at[one_rows(1 - x, y), right], attn_last_b, here.to_x),
+    ]
+    def settle_attn():
+        get_slope_attn.wait()
+        for copy in attn_second:
+            copy.wait_recv()
+
+        @pl.loop(0, share // step)
+        def _(index):
+            flat = pl.ds(mul(index, step), step)
+            at = pl.ds(pl.multiple_of(here.slot(x, core, y) * share + index * step, step), step)
+            came = pl.ds(pl.multiple_of(y * share + index * step, step), step)
+            mine = ea[at, left].astype(F32) + attn_a[came, :].astype(F32)
+            mine = mine + attn_last_a[flat, :].astype(F32)
+            ea[at, left] = (mine * slope_attn[flat, left].astype(F32)).astype(BF16)
+            mine = ea[at, right].astype(F32) + attn_b[x, flat, :].astype(F32)
+            mine = mine + attn_last_b[flat, :].astype(F32)
+            ea[at, right] = (mine * slope_attn[flat, right].astype(F32)).astype(BF16)
+
+        ends.append(fetch(ea.at[one_rows(x, y)], out_attn))
+
+    ends = []
+    for tick in tok_ticks:
+        output_wave(17 + next(count))
+        if tick > 9:
+            next(gain_waves, None)
+        if tick == 10:
+            ends.append(fetch(own_ffn, mixed_out.at[chunk_rows]))
+            ends.append(fetch(own_tokens, tokens_out.at[chunk_rows]))
+        if tick == 11:
+            settle(0)
+        if tick == 12:
+            settle_attn()
+    for tick in ffn_ticks:
+        pass
+    for _ in gain_waves:
+        pass
+    ends.append(fetch(gain_sum.at[2], gains_out))
+    ffn_line.close()
+    tok_line.close()
+    for keep, give in ending:
+        give.wait_recv()
+    for keep, give in ending[1:]:
+        keep.wait()
+    mail.close()
+    for copy in ends:
+        copy.wait()
+
+
+def back(given, x1, small, attn, tokens, cotangent, segments, slope_ffn, slope_attn):
+    rows, width = tokens.shape
+    half = given[2].shape[1]
+    share = width // 8
+    e_attn, query, kv = attn[0], attn[1], attn[2]
+    n_attn, n_query, n_kv = e_attn.shape[1], query.shape[1], kv.shape[1]
+    cut = 3 * n_attn // 4
+    chunk = rows // 4
+    shapes = [
+        *[((share, 2 * half), BF16)] * 3,
+        ((share, n_attn), BF16),
+        ((rows, width), BF16),
+        ((rows, width), BF16),
+        ((2, width), F32),
+        *[((width, half), BF16)] * 3,
+    ]
+    in_vmem = pl.BlockSpec(memory_space=pltpu.VMEM)
+    anywhere = pl.BlockSpec(memory_space=pl.ANY)
+    scratch = [
+        pltpu.VMEM((2, 2 * share, half), BF16),
+        pltpu.VMEM((2, 2, share, half), BF16),
+        pltpu.VMEM((3, 2 * share, half), BF16),
+        pltpu.VMEM((3, 2, share, half), BF16),
+        pltpu.VMEM((3, share, half), BF16),
+        pltpu.VMEM((3, share, half), BF16),
+        pltpu.VMEM((2, share, half), BF16),
+        pltpu.VMEM((rows, width), BF16),
+        pltpu.VMEM((rows, width), BF16),
+        pltpu.VMEM((rows, width), BF16),
+        pltpu.VMEM((chunk, width), BF16),
+        pltpu.VMEM((chunk, width), BF16),
+        pltpu.VMEM((2, 3, chunk, width), BF16),
+        pltpu.VMEM((2, 3, chunk, width), BF16),
+        pltpu.VMEM((chunk // BACK_SUBS, width), F32),
+        pltpu.VMEM((width, n_attn), BF16),
+        pltpu.VMEM((2, 2 * share, n_attn), BF16),
+        pltpu.VMEM((2 * share, cut), BF16),
+        pltpu.VMEM((2, share, n_attn - cut), BF16),
+        pltpu.VMEM((share, cut), BF16),
+        pltpu.VMEM((share, n_attn - cut), BF16),
+        pltpu.VMEM((rows + EXTRA, n_query), BF16),
+        pltpu.VMEM((rows + EXTRA, n_kv), BF16),
+        pltpu.VMEM((rows, n_query), BF16),
+        pltpu.VMEM((rows, width), BF16),
+        pltpu.VMEM((rows + EXTRA, 128), F32),
+        pltpu.VMEM((rows, n_query + n_kv), BF16),
+        pltpu.VMEM((rows + EXTRA, n_kv), F32),
+        pltpu.VMEM((EXTRA, n_query), BF16),
+        pltpu.VMEM((EXTRA, n_query), BF16),
+        pltpu.VMEM((EXTRA, n_query + n_kv), BF16),
+        pltpu.VMEM((EXTRA, n_query + n_kv), BF16),
+        pltpu.VMEM((chunk, width), F32),
+        pltpu.VMEM((chunk, width), F32),
+        pltpu.VMEM((chunk, width), BF16),
+        pltpu.VMEM((chunk, width), BF16),
+        pltpu.VMEM((2, width), F32),
+        pltpu.VMEM((3, 2, width), F32),
+        pltpu.VMEM((9, 2, width), F32),
+        *line_sems(BACK_SUBS),
+        *line_sems(BACK_SUBS),
+        pltpu.SemaphoreType.DMA((3, 2)),
+        pltpu.SemaphoreType.DMA((36,)),
+        pltpu.SemaphoreType.DMA((31,)),
+        pltpu.SemaphoreType.DMA((31,)),
+    ]
+    places = [anywhere] * 9 + [in_vmem] + [anywhere] * 7 + [in_vmem] + [anywhere] * 2
+    return pl.pallas_call(
+        back_kernel,
+        out_shape=[jax.ShapeDtypeStruct(s, d) for s, d in shapes],
+        in_specs=places,
+        out_specs=[anywhere] * len(shapes),
+        scratch_shapes=scratch,
+        compiler_params=pltpu.CompilerParams(
+            collective_id=1, has_side_effects=True, vmem_limit_bytes=VMEM_BYTES
+        ),
+        cost_estimate=pl.CostEstimate(
+            flops=26 * 10**9, bytes_accessed=120 * 10**6, transcendentals=4 * 10**6
+        ),
+        name="back",
+    )(*given, x1, small, *attn, tokens, cotangent, segments, slope_ffn, slope_attn)
+
+
+def end_kernel(
+    mixed_in,
+    tokens_in,
+    gate_in,
+    up_in,
+    attn_in,
+    down_in,
+    small,
+    peaks,
+    gain_sum,
+    mixed,
+    tokens,
+    query,
+    key,
+    value,
+    out,
+    gate,
+    up,
+    down,
+    attn_scales,
+    kv_scales,
+    ffn_scales,
+    gain_one,
+    gain_two,
+    tall_in,
+    tall_out,
+    wide_in,
+    wide_out,
+    attn_b,
+    attn_f,
+    down_b,
+    down_f,
+    turned,
+    in_sem,
+    out_sem,
+):
+    n_query, n_key = query.shape[1], key.shape[1]
+    n_in = n_query + 2 * n_key
+    step = 32
+    reads = [
+        (mixed_in, tall_in.at[0]),
+        (tokens_in, tall_in.at[1]),
+        (down_in, down_b),
+        (gate_in, wide_in.at[0]),
+        (up_in, wide_in.at[1]),
+        (attn_in, attn_b),
+    ]
+    reads = [pltpu.make_async_copy(a, b, in_sem.at[i]) for i, (a, b) in enumerate(reads)]
+    for copy in reads:
+        copy.start()
+    writes = []
+
+    def write(src, dst):
+        copy = pltpu.make_async_copy(src, dst, out_sem.at[len(writes)])
+        copy.start()
+        writes.append(copy)
+
+    def widen(src, dst):
+        @pl.loop(0, src.shape[0] // step)
+        def _(index):
+            at = pl.ds(mul(index, step), step)
+            dst[at, :] = src[at, :].astype(F32)
+
+    for i, target in enumerate((mixed, tokens)):
+        reads[i].wait()
+        widen(tall_in.at[i], tall_out.at[i])
+        write(tall_out.at[i], target)
+    reads[2].wait()
+    widen(down_b, down_f)
+    write(down_f, down)
+    for i, target in enumerate((gate, up)):
+        reads[3 + i].wait()
+        widen(wide_in.at[i], wide_out.at[i])
+        write(wide_out.at[i], target)
+    reads[5].wait()
+    widen(attn_b, attn_f)
+    write(attn_f.at[:, pl.ds(0, n_query)], query)
+    write(attn_f.at[:, pl.ds(n_query, n_key)], key)
+    write(attn_f.at[:, pl.ds(n_query + n_key, n_key)], value)
+    write(attn_f.at[:, pl.ds(n_in, n_query)], out)
+    piece = small.shape[1]
+    for row, first in enumerate((0, n_in)):
+        for i in range(n_query // piece):
+            at = first // piece + i
+            attn_scales[row : row + 1, i * piece : (i + 1) * piece] = small[at : at + 1, :]
+    for row in (0, 1):
+        for i in range(n_key // piece):
+            at = (n_query + row * n_key) // piece + i
+            kv_scales[row : row + 1, i * piece : (i + 1) * piece] = small[at : at + 1, :]
+    ffn_scales[...] = peaks[0:3, :]
+    share, width = gain_one.shape[0], gain_sum.shape[1]
+    slot = lax.axis_index("dp") * 2 + lax.axis_index("seq")
+    turned[...] = jnp.zeros_like(turned)
+    turned[0:2, :] = gain_sum[...]
+    turned[...] = pltpu.roll(turned[...], lax.rem(width - slot * share, width), 1)
+    gain_one[...] = turned[0, :share]
+    gain_two[...] = turned[1, :share]
+    for copy in writes:
+        copy.wait()
+
+
+def end(mixed_b, tokens_b, sum_gate, sum_up, sum_attn, sum_down, small, peaks, gain_sum, n_query):
+    rows, width = mixed_b.shape
+    share, hidden = sum_gate.shape
+    n_attn = sum_attn.shape[1]
+    n_key = (n_attn - 2 * n_query) // 2
+    shapes = [
+        (rows, width),
+        (rows, width),
+        (share, n_query),
+        (share, n_key),
+        (share, n_key),
+        (share, n_query),
+        (share, hidden),
+        (share, hidden),
+        (share, hidden),
+        (2, n_query),
+        (2, n_key),
+        (3, hidden),
+        (share,),
+        (share,),
+    ]
+    in_vmem = pl.BlockSpec(memory_space=pltpu.VMEM)
+    anywhere = pl.BlockSpec(memory_space=pl.ANY)
+    return pl.pallas_call(
+        end_kernel,
+        out_shape=[jax.ShapeDtypeStruct(s, F32) for s in shapes],
+        in_specs=[anywhere] * 6 + [in_vmem] * 3,
+        out_specs=[anywhere] * 9 + [in_vmem] * 5,
+        scratch_shapes=[
+            pltpu.VMEM((2, rows, width), BF16),
+            pltpu.VMEM((2, rows, width), F32),
+            pltpu.VMEM((2, share, hidden), BF16),
+            pltpu.VMEM((2, share, hidden), F32),
+            pltpu.VMEM((share, n_attn), BF16),
+            pltpu.VMEM((share, n_attn), F32),
+            pltpu.VMEM((share, hidden), BF16),
+            pltpu.VMEM((share, hidden), F32),
+            pltpu.VMEM((8, width), F32),
+            pltpu.SemaphoreType.DMA((6,)),
+            pltpu.SemaphoreType.DMA((9,)),
+        ],
+        compiler_params=pltpu.CompilerParams(vmem_limit_bytes=VMEM_BYTES),
+        cost_estimate=pl.CostEstimate(flops=0, bytes_accessed=29 * 10**6, transcendentals=0),
+        name="end",
+    )(mixed_b, tokens_b, sum_gate, sum_up, sum_attn, sum_down, small, peaks, gain_sum)
+
+
+def paired_block(
+    tokens,
+    gain_attn,
+    w_query,
+    w_key,
+    w_value,
+    w_out,
+    gain_ffn,
+    w_gate,
+    w_up,
+    w_down,
+    width_pick,
+    segments,
+    cotangent,
+):
+    dp, y = lax.axis_index("dp"), lax.axis_index("seq")
+    n_query = w_query.shape[1]
+    slot = dp * 2 + y
+    mine = jnp.arange(8, dtype=jnp.int32)[:, None] == slot
+    gains = [jnp.where(mine, g[None, :], 0) for g in (gain_attn, gain_ffn)]
+    gains = jnp.pad(jnp.stack(gains).reshape(-1, 256), ((8, 6), (0, 0)))
+    weights = (w_query, w_key, w_value, w_out.T, w_down.T, w_gate, w_up)
+    (
+        e_attn,
+        hidden_two,
+        resid,
+        query_b,
+        kv,
+        heads_b,
+        hidden_one,
+        cot_other,
+        mixed_in,
+        grad_gate_b,
+        grad_up_b,
+        back_part,
+        ffn_part,
+        slope_ffn,
+        slope_attn,
+        small,
+        peaks,
+        early,
+    ) = front(width_pick, weights, gains, tokens, cotangent, segments)
+    sum_down, sum_gate, sum_up, sum_attn, mixed_b, tokens_b, gain_sum, _, _, _ = back(
+        (back_part, ffn_part, mixed_in, grad_gate_b, grad_up_b, hidden_two, cot_other, early),
+        resid,
+        small,
+        (e_attn, query_b, kv, heads_b, hidden_one),
+        tokens,
+        cotangent,
+        segments,
+        slope_ffn,
+        slope_attn,
+    )
+    mixed, grad_tokens, g_query, g_key, g_value, g_out, g_gate, g_up, g_down, *scales, gain_one, gain_two = end(
+        mixed_b, tokens_b, sum_gate, sum_up, sum_attn, sum_down, small, peaks, gain_sum, n_query
+    )
+    return (
+        mixed,
+        grad_tokens,
+        g_query,
+        g_key,
+        g_value,
+        g_out.T,
+        g_gate,
+        g_up,
+        g_down.T,
+        gain_one,
+        gain_two,
+        *scales,
+    )
+
+
 def solution(mesh):
     in_specs = (
         P(("dp", "seq"), None),
@@ -307,6 +2170,9 @@
         P(None, "mp"),
         P(None, "mp"),
     )
+    shape = dict(mesh.shape)
+    paired = shape["dp"] == 4 and shape["seq"] == 2 and shape["mp"] == 4
+    block = paired_block if paired else on_device
     return jax.shard_map(
-        on_device, mesh=mesh, in_specs=in_specs, out_specs=out_specs, check_vma=False
-    )
+        block, mesh=mesh, in_specs=in_specs, out_specs=out_specs, check_vma=False
+    )

time: 1690 us -> 387 us (0.23)
  waiting for transfers between devices: 1310 us -> 0 us
  Pallas kernels: 0 us -> 379 us
  matrix products: 154 us -> 0 us
  blocking collectives: 91.9 us -> 0 us
  other arithmetic: 86.4 us -> 0.79 us
  local copies, waits for them, and re-layouts: 21.8 us -> 0.71 us
    psum x4 -> x0, waiting for transfers between devices: 593 us -> none  [the longest x1 172 us: on_device(): lax.psum(against(grad_query_b, eff_query) + against(grad_key_b, eff_key)...]
    reduce_scatter x9 -> x0, waiting for transfers between devices: 541 us -> none  [the longest x1 139 us: on_device(): lax.psum_scatter(grad_down_eff, ('dp', 'seq'), scatter_dimension=1, tiled...]
    pallas_call x0 -> x3, Pallas kernels: none -> 379 us  [the longest x1 185 us: back(): pl.pallas_call(back_kernel, out_shape=[jax.ShapeDtypeStruct(s, d) for s,...]
    all_gather x7 -> x0, waiting for transfers between devices: 171 us -> none  [the longest x1 58.9 us: on_device(): lax.all_gather(w_up, ('dp', 'seq'), axis=0, tiled=True)]
    dot_general x27 -> x0, matrix products: 154 us -> none  [the longest x7 54 us: inner_rows(): lax.dot_general(left, right, (((0,), (0,)), ((), ())), preferred_element_...]
    unnamed x2 -> x0, blocking collectives: 47.2 us -> none
    pmax x1 -> x0, blocking collectives: 25.8 us -> none  [on_device(): lax.pmax(channel_peak(w_query, 0).astype(jnp.bfloat16), ('dp', 'seq'))]
    mul x14 -> x0, other arithmetic: 23.8 us -> none  [the longest x1 4.14 us: on_device(): grad_down = sum_down * bound_slope(w_down, bound_down)]
  transfers between devices with their start and end apart: 20 -> 0, of which waited for: 16 -> 0; matrix products, arithmetic and copies ran while one was open for 11% -> 0% of each run, Pallas kernels for 0% -> 0%
where the time goes in v2:
time: 387 us; the launch traced here: 382 us
  Pallas kernels  379 us (98%)
    pallas_call x1, Pallas kernels, back(): pl.pallas_call(back_kernel, out_shape=[jax.ShapeDtypeStruct(s, d) for s,...  185 us
    pallas_call x1, Pallas kernels, front(): pl.pallas_call(front_kernel, out_shape=[jax.ShapeDtypeStruct(s, d) for s,...  183 us
    pallas_call x1, Pallas kernels, end(): pl.pallas_call(end_kernel, out_shape=[jax.ShapeDtypeStruct(s, F32) for s...  10.5 us

profile of v2, /device:TPU:0, one launch (start us, length us, event | category | flops | bytes accessed | tf_op | source)
XLA Modules:
  0.0 381.7 jit_solution(5308241462519596766)
XLA Ops:
  0.7 0.8 broadcast_select_fusion.1
  1.4 0.1 reshape.124
  1.5 0.6 pad.4.gains
  2.2 183.3 %front.1 = (bf16[2304,1536]{1,0:T(8,128)(2,1)}, bf16[1024,2304]{1,0:T(8,128)(2,1)}, f32[128,2304]{1,0:T(8,128)}, bf16[528,512]{1,0:T(8,128)(2,1)}, bf16[528,512]...) custom-call(s32[7]{0:T(128)} %width_pick.1, ...), custom_call_target="tpu_custom_call" | custom-call | flops 35999997952 | bytes 90000000 | tf_op jit(solution)/shard_map/front/pallas_call | solution.py:1182
  185.5 185.5 %back.1 = (bf16[288,2304]{1,0:T(8,128)(2,1)}, bf16[288,2304]{1,0:T(8,128)(2,1)}, bf16[288,2304]{1,0:T(8,128)(2,1)}, bf16[288,1536]{1,0:T(8,128)(2,1)}, bf16[512,...) custom-call(bf16[1024,2304]{1,0:T(8,128)(2,1)} %get-tuple-element.53, ...), custom_call_target="tpu_custom_call" | custom-call | flops 25999998976 | bytes 120000000 | tf_op jit(solution)/shard_map/back/pallas_call | solution.py:1905
  370.9 10.5 %end.1 = (f32[512,2304]{1,0:T(8,128)}, f32[512,2304]{1,0:T(8,128)}, f32[288,512]{1,0:T(8,128)}, f32[288,256]{1,0:T(8,128)}, f32[288,256]{1,0:T(8,128)}, /*index=...) custom-call(bf16[512,2304]{1,0:T(8,128)(2,1)} %get-tuple-element.70., ...), custom_call_target="tpu_custom_call" | custom-call | bytes 29000000 | tf_op jit(solution)/shard_map/end/pallas_call | solution.py:2045
  (2 shorter events, 0.0 us)

commit v3 on v2

--- a/solution.py
+++ b/solution.py
@@ -602,7 +602,8 @@
     w_down_t,
     w_gate,
     w_up,
-    gains,
+    gain_attn,
+    gain_ffn,
     tokens_in,
     cot_in,
     segments,
@@ -641,6 +642,7 @@
     grad_gate,
     grad_up,
     slope_attn,
+    turned,
     small_src,
     small_land,
     small,
@@ -716,7 +718,16 @@
     attn_peak = peak(ea[own_rows, :])
     piece = small_src.shape[1]
     n_pieces = n_attn // piece
-    small_src[...] = gains[...].astype(F32)
+    turned[...] = jnp.zeros_like(turned)
+    turned[0, :share] = gain_attn[...].astype(F32)
+    turned[1, :share] = gain_ffn[...].astype(F32)
+    turned[...] = pltpu.roll(turned[...], own_at, 1)
+    small_src[...] = jnp.zeros_like(small_src)
+    for row in (0, 1):
+        for index in range(width // piece):
+            to = 8 + row * (width // piece) + index
+            at = slice(index * piece, (index + 1) * piece)
+            small_src[to : to + 1, :] = turned[row : row + 1, at]
     for index in range(n_pieces):
         at = slice(index * piece, (index + 1) * piece)
         small_src[index : index + 1, :] = attn_peak[:, at]
@@ -1114,7 +1125,7 @@
         copy.wait()
 
 
-def front(width_pick, weights, gains, tokens, cotangent, segments):
+def front(width_pick, weights, gain_attn, gain_ffn, tokens, cotangent, segments):
     rows, width = tokens.shape
     share, n_query = weights[0].shape
     n_kv = 2 * weights[1].shape[1]
@@ -1162,6 +1173,7 @@
         pltpu.VMEM((2 * rows, half), BF16),
         pltpu.VMEM((2 * rows, half), BF16),
         pltpu.VMEM((share, n_attn), BF16),
+        pltpu.VMEM((8, width), F32),
         pltpu.VMEM((32, 256), F32),
         pltpu.VMEM((4, 32, 256), F32),
         pltpu.VMEM((32, 256), F32),
@@ -1182,7 +1194,7 @@
     return pl.pallas_call(
         front_kernel,
         out_shape=[jax.ShapeDtypeStruct(s, d) for s, d in shapes],
-        in_specs=[in_smem] + [anywhere] * 7 + [in_vmem, anywhere, anywhere, in_vmem],
+        in_specs=[in_smem] + [anywhere] * 7 + [in_vmem] * 2 + [anywhere] * 2 + [in_vmem],
         out_specs=[anywhere] * len(shapes),
         scratch_shapes=scratch,
         compiler_params=pltpu.CompilerParams(
@@ -1192,7 +1204,7 @@
             flops=36 * 10**9, bytes_accessed=90 * 10**6, transcendentals=8 * 10**6
         ),
         name="front",
-    )(width_pick, *weights, gains, tokens, cotangent, segments)
+    )(width_pick, *weights, gain_attn, gain_ffn, tokens, cotangent, segments)
 
 
 OUTPUT_PLAN = (7, 8, 10, 11, 12, 14, 15, 17, 18, 19, 20, 21, 22, 23)
@@ -1679,9 +1691,6 @@
     ship_all(0, 0, (1,))
     ship_all(0, 1)
     output_wave(15)
-    settle(1)
-    get_slopes(2)
-    restage(0, 1)
     row_copy.wait_recv()
     at = pl.ds(edge(y, rows), EXTRA)
     grad_in[at, :n_query] = (grad_in[at, :n_query].astype(F32) + row_land[:, :n_query].astype(F32)).astype(BF16)
@@ -1705,6 +1714,9 @@
     next(tok_ticks, None)
     output_wave(18)
     relay(2)
+    settle(1)
+    get_slopes(2)
+    restage(0, 1)
     get_h1.wait()
 
     @pl.loop(0, width // tile)
@@ -1925,9 +1937,9 @@
     up_in,
     attn_in,
     down_in,
-    small,
-    peaks,
-    gain_sum,
+    small_in,
+    peaks_in,
+    gains_in,
     mixed,
     tokens,
     query,
@@ -1937,6 +1949,14 @@
     gate,
     up,
     down,
+    attn_out,
+    kv_out,
+    ffn_out,
+    one_out,
+    two_out,
+    small,
+    peaks,
+    gain_sum,
     attn_scales,
     kv_scales,
     ffn_scales,
@@ -1964,6 +1984,9 @@
         (gate_in, wide_in.at[0]),
         (up_in, wide_in.at[1]),
         (attn_in, attn_b),
+        (small_in, small),
+        (peaks_in, peaks),
+        (gains_in, gain_sum),
     ]
     reads = [pltpu.make_async_copy(a, b, in_sem.at[i]) for i, (a, b) in enumerate(reads)]
     for copy in reads:
@@ -1985,19 +2008,8 @@
         reads[i].wait()
         widen(tall_in.at[i], tall_out.at[i])
         write(tall_out.at[i], target)
-    reads[2].wait()
-    widen(down_b, down_f)
-    write(down_f, down)
-    for i, target in enumerate((gate, up)):
-        reads[3 + i].wait()
-        widen(wide_in.at[i], wide_out.at[i])
-        write(wide_out.at[i], target)
-    reads[5].wait()
-    widen(attn_b, attn_f)
-    write(attn_f.at[:, pl.ds(0, n_query)], query)
-    write(attn_f.at[:, pl.ds(n_query, n_key)], key)
-    write(attn_f.at[:, pl.ds(n_query + n_key, n_key)], value)
-    write(attn_f.at[:, pl.ds(n_in, n_query)], out)
+    for copy in reads[6:]:
+        copy.wait()
     piece = small.shape[1]
     for row, first in enumerate((0, n_in)):
         for i in range(n_query // piece):
@@ -2015,6 +2027,27 @@
     turned[...] = pltpu.roll(turned[...], lax.rem(width - slot * share, width), 1)
     gain_one[...] = turned[0, :share]
     gain_two[...] = turned[1, :share]
+    for src, dst in (
+        (attn_scales, attn_out),
+        (kv_scales, kv_out),
+        (ffn_scales, ffn_out),
+        (gain_one, one_out),
+        (gain_two, two_out),
+    ):
+        write(src, dst)
+    reads[2].wait()
+    widen(down_b, down_f)
+    write(down_f, down)
+    for i, target in enumerate((gate, up)):
+        reads[3 + i].wait()
+        widen(wide_in.at[i], wide_out.at[i])
+        write(wide_out.at[i], target)
+    reads[5].wait()
+    widen(attn_b, attn_f)
+    write(attn_f.at[:, pl.ds(0, n_query)], query)
+    write(attn_f.at[:, pl.ds(n_query, n_key)], key)
+    write(attn_f.at[:, pl.ds(n_query + n_key, n_key)], value)
+    write(attn_f.at[:, pl.ds(n_in, n_query)], out)
     for copy in writes:
         copy.wait()
 
@@ -2040,14 +2073,15 @@
         (share,),
         (share,),
     ]
-    in_vmem = pl.BlockSpec(memory_space=pltpu.VMEM)
     anywhere = pl.BlockSpec(memory_space=pl.ANY)
     return pl.pallas_call(
         end_kernel,
         out_shape=[jax.ShapeDtypeStruct(s, F32) for s in shapes],
-        in_specs=[anywhere] * 6 + [in_vmem] * 3,
-        out_specs=[anywhere] * 9 + [in_vmem] * 5,
+        in_specs=[anywhere] * 9,
+        out_specs=[anywhere] * 14,
         scratch_shapes=[
+            *(pltpu.VMEM(a.shape, F32) for a in (small, peaks, gain_sum)),
+            *(pltpu.VMEM(shape, F32) for shape in shapes[9:]),
             pltpu.VMEM((2, rows, width), BF16),
             pltpu.VMEM((2, rows, width), F32),
             pltpu.VMEM((2, share, hidden), BF16),
@@ -2057,8 +2091,8 @@
             pltpu.VMEM((share, hidden), BF16),
             pltpu.VMEM((share, hidden), F32),
             pltpu.VMEM((8, width), F32),
-            pltpu.SemaphoreType.DMA((6,)),
             pltpu.SemaphoreType.DMA((9,)),
+            pltpu.SemaphoreType.DMA((14,)),
         ],
         compiler_params=pltpu.CompilerParams(vmem_limit_bytes=VMEM_BYTES),
         cost_estimate=pl.CostEstimate(flops=0, bytes_accessed=29 * 10**6, transcendentals=0),
@@ -2081,12 +2115,7 @@
     segments,
     cotangent,
 ):
-    dp, y = lax.axis_index("dp"), lax.axis_index("seq")
     n_query = w_query.shape[1]
-    slot = dp * 2 + y
-    mine = jnp.arange(8, dtype=jnp.int32)[:, None] == slot
-    gains = [jnp.where(mine, g[None, :], 0) for g in (gain_attn, gain_ffn)]
-    gains = jnp.pad(jnp.stack(gains).reshape(-1, 256), ((8, 6), (0, 0)))
     weights = (w_query, w_key, w_value, w_out.T, w_down.T, w_gate, w_up)
     (
         e_attn,
@@ -2107,7 +2136,7 @@
         small,
         peaks,
         early,
-    ) = front(width_pick, weights, gains, tokens, cotangent, segments)
+    ) = front(width_pick, weights, gain_attn, gain_ffn, tokens, cotangent, segments)
     sum_down, sum_gate, sum_up, sum_attn, mixed_b, tokens_b, gain_sum, _, _, _ = back(
         (back_part, ffn_part, mixed_in, grad_gate_b, grad_up_b, hidden_two, cot_other, early),
         resid,

time: 387 us -> 385 us (level)
  no operation moved by 1% of the time
where the time goes in v3:
time: 385 us; the launch traced here: 380 us
  Pallas kernels  379 us (98%)
    pallas_call x1, Pallas kernels, back(): pl.pallas_call(back_kernel, out_shape=[jax.ShapeDtypeStruct(s, d) for s,...  186 us
    pallas_call x1, Pallas kernels, front(): pl.pallas_call(front_kernel, out_shape=[jax.ShapeDtypeStruct(s, d) for s,...  183 us
    pallas_call x1, Pallas kernels, end(): pl.pallas_call(end_kernel, out_shape=[jax.ShapeDtypeStruct(s, F32) for s...  9.79 us

profile of v3, /device:TPU:0, one launch (start us, length us, event | category | flops | bytes accessed | tf_op | source)
XLA Modules:
  0.0 379.8 jit_solution(13231114366672487735)
XLA Ops:
  0.6 183.5 %front.1 = (bf16[2304,1536]{1,0:T(8,128)(2,1)}, bf16[1024,2304]{1,0:T(8,128)(2,1)}, f32[128,2304]{1,0:T(8,128)}, bf16[528,512]{1,0:T(8,128)(2,1)}, bf16[528,512]...) custom-call(s32[7]{0:T(128)} %width_pick.1, ...), custom_call_target="tpu_custom_call" | custom-call | flops 35999997952 | bytes 90000000 | tf_op jit(solution)/shard_map/front/pallas_call | solution.py:1194
  184.1 185.7 %back.1 = (bf16[288,2304]{1,0:T(8,128)(2,1)}, bf16[288,2304]{1,0:T(8,128)(2,1)}, bf16[288,2304]{1,0:T(8,128)(2,1)}, bf16[288,1536]{1,0:T(8,128)(2,1)}, bf16[512,...) custom-call(bf16[1024,2304]{1,0:T(8,128)(2,1)} %get-tuple-element.53, ...), custom_call_target="tpu_custom_call" | custom-call | flops 25999998976 | bytes 120000000 | tf_op jit(solution)/shard_map/back/pallas_call | solution.py:1917
  369.8 9.8 %end.1 = (f32[512,2304]{1,0:T(8,128)}, f32[512,2304]{1,0:T(8,128)}, f32[288,512]{1,0:T(8,128)}, f32[288,256]{1,0:T(8,128)}, f32[288,256]{1,0:T(8,128)}, /*index=...) custom-call(bf16[512,2304]{1,0:T(8,128)(2,1)} %get-tuple-element.70., ...), custom_call_target="tpu_custom_call" | custom-call | bytes 29000000 | tf_op jit(solution)/shard_map/end/pallas_call | solution.py:2077

commit v4 on v3

--- a/solution.py
+++ b/solution.py
@@ -1057,6 +1057,8 @@
             back_into_mixed(0)
     line.close()
     outs.append(fetch(x1, x1_out))
+    peer_copy.wait_recv()
+    outs.append(fetch(peaks_peer, peaks_out.at[:, their_cols]))
     arrived(1, 0)
     arrived(2, 0)
     all_given.wait_recv()
@@ -1118,8 +1120,6 @@
 
     to_width(ffn_part, downward, 2, ffn_leaves)
     cot_keep.wait()
-    peer_copy.wait_recv()
-    outs.append(fetch(peaks_peer, peaks_out.at[:, their_cols]))
     mail.close()
     for copy in outs:
         copy.wait()
@@ -1767,7 +1767,7 @@
         output_wave(17 + next(count))
 
     def gain_steps():
-        rounds = (plane, [near_target], [far_target])
+        rounds = ([near_target], [far_target], plane)
         mine, at = gain_part, 0
         for number, targets in enumerate(rounds):
             places = gain_land.at[pl.ds(at, len(targets))]

time: 385 us -> 385 us (level)
  no operation moved by 1% of the time
where the time goes in v4:
time: 385 us; the launch traced here: 380 us
  Pallas kernels  379 us (98%)
    pallas_call x1, Pallas kernels, back(): pl.pallas_call(back_kernel, out_shape=[jax.ShapeDtypeStruct(s, d) for s,...  186 us
    pallas_call x1, Pallas kernels, front(): pl.pallas_call(front_kernel, out_shape=[jax.ShapeDtypeStruct(s, d) for s,...  183 us
    pallas_call x1, Pallas kernels, end(): pl.pallas_call(end_kernel, out_shape=[jax.ShapeDtypeStruct(s, F32) for s...  9.79 us

profile of v4, /device:TPU:0, one launch (start us, length us, event | category | flops | bytes accessed | tf_op | source)
XLA Modules:
  0.0 379.9 jit_solution(17790737525986671180)
XLA Ops:
  0.6 183.4 %front.1 = (bf16[2304,1536]{1,0:T(8,128)(2,1)}, bf16[1024,2304]{1,0:T(8,128)(2,1)}, f32[128,2304]{1,0:T(8,128)}, bf16[528,512]{1,0:T(8,128)(2,1)}, bf16[528,512]...) custom-call(s32[7]{0:T(128)} %width_pick.1, ...), custom_call_target="tpu_custom_call" | custom-call | flops 35999997952 | bytes 90000000 | tf_op jit(solution)/shard_map/front/pallas_call | solution.py:1194
  184.1 185.8 %back.1 = (bf16[288,2304]{1,0:T(8,128)(2,1)}, bf16[288,2304]{1,0:T(8,128)(2,1)}, bf16[288,2304]{1,0:T(8,128)(2,1)}, bf16[288,1536]{1,0:T(8,128)(2,1)}, bf16[512,...) custom-call(bf16[1024,2304]{1,0:T(8,128)(2,1)} %get-tuple-element.53, ...), custom_call_target="tpu_custom_call" | custom-call | flops 25999998976 | bytes 120000000 | tf_op jit(solution)/shard_map/back/pallas_call | solution.py:1917
  369.9 9.8 %end.1 = (f32[512,2304]{1,0:T(8,128)}, f32[512,2304]{1,0:T(8,128)}, f32[288,512]{1,0:T(8,128)}, f32[288,256]{1,0:T(8,128)}, f32[288,256]{1,0:T(8,128)}, /*index=...) custom-call(bf16[512,2304]{1,0:T(8,128)(2,1)} %get-tuple-element.70., ...), custom_call_target="tpu_custom_call" | custom-call | bytes 29000000 | tf_op jit(solution)/shard_map/end/pallas_call | solution.py:2077
